TPU v7x, 32 devices: a whole 2x2x4 slice. The times are simulated.
32 devices in a mesh: wall: 4 (over z), span: 4 (over y, x), stream: 2 (over core).
Axes of the slice: x: 2, y: 2, z: 4, core: 2. Of those that a mesh axis runs over, the one named last changes fastest.
Arguments:
- conserved: float32 [5, 32, 384, 512], P(None, 'stream', 'wall', 'span'), may hold values from -6 to 6
- wall_metric: float32 [32, 384, 512], P('stream', 'wall', 'span'), may hold values from 0.5 to 4
- span_metric: float32 [32, 384, 512], P('stream', 'wall', 'span'), may hold values from 0.5 to 4
Outputs:
- wall_slope: float32 [5, 32, 384, 512], P(None, 'stream', 'wall', 'span')
- span_slope: float32 [5, 32, 384, 512], P(None, 'stream', 'wall', 'span')
All inputs are finite; a program needn't handle non-finite values.
Results may differ from a plain program's by a relative error of at most 0.0003.
Values sent between devices are 32-bit elements; how exact they have to be, the bound alone decides.
A program may use at most 128 MiB of HBM per device.

v0:
```python
import jax
import jax.numpy as jnp
import numpy as np
from jax import lax
from jax.sharding import PartitionSpec as P

HIGHEST_MODE = lax.Precision.HIGHEST
band_alpha = 0.4995


def line_coefficients(length_all):
    lower_band = np.full(length_all, band_alpha)
    lower_band[1] = 0.25
    lower_band[length_all - 2] = 0.25
    lower_band[0] = 0.0
    lower_band[length_all - 1] = 0.0
    scales = np.zeros(length_all)
    pivots = np.zeros(length_all)
    previous = 0.0
    for row_idx in range(length_all):
        scales[row_idx] = 1.0 / (1.0 - lower_band[row_idx] * previous)
        pivots[row_idx] = lower_band[row_idx] * scales[row_idx]
        previous = pivots[row_idx]
    near_coef = (band_alpha + 2.0) / 3.0
    far_coef = (4.0 * band_alpha - 1.0) / 12.0
    weights = np.zeros((5, length_all))
    weights[:, :] = np.array([-far_coef, -near_coef, 0.0, near_coef, far_coef])[:, None]
    weights[:, 1] = [0.0, -0.75, 0.0, 0.75, 0.0]
    weights[:, length_all - 2] = [0.0, -0.75, 0.0, 0.75, 0.0]
    weights[:, 0] = [0.0, 0.0, -1.5, 2.0, -0.5]
    weights[:, length_all - 1] = [0.5, -2.0, 1.5, 0.0, 0.0]
    return (lower_band, scales, pivots, weights)


def block_tables(pieces, block_len):
    length_all = pieces * block_len
    lower_band, scales, pivots, weights = line_coefficients(length_all)
    down_maps = np.zeros((pieces, block_len, block_len))
    enter_gain = np.zeros((pieces, block_len))
    back_maps = np.zeros((pieces, block_len, block_len))
    leave_gain = np.zeros((pieces, block_len))
    for piece_idx in range(pieces):
        base_row = piece_idx * block_len
        row_now = np.zeros(block_len)
        running = 1.0
        for step_idx in range(block_len):
            factor = -lower_band[base_row + step_idx] * scales[base_row + step_idx]
            row_now = factor * row_now
            row_now[step_idx] += 1.0
            down_maps[piece_idx, step_idx] = row_now * scales[base_row : base_row + block_len]
            running = factor * running
            enter_gain[piece_idx, step_idx] = running
        row_now = np.zeros(block_len)
        running = 1.0
        for step_idx in range(block_len - 1, -1, -1):
            factor = -pivots[base_row + step_idx]
            row_now = factor * row_now
            row_now[step_idx] += 1.0
            back_maps[piece_idx, step_idx] = row_now
            running = factor * running
            leave_gain[piece_idx, step_idx] = running
    return tuple(
        (
            jnp.asarray(table, jnp.float32)
            for table in (weights, down_maps, enter_gain, back_maps, leave_gain)
        )
    )


def compose(earlier, later):
    return (later[0] * earlier[0], later[0] * earlier[1] + later[1])


def stencil(padded, weights, block_len, line_dim):
    right_side = 0.0
    for offset in range(5):
        shifted = lax.slice_in_dim(padded, offset, offset + block_len, axis=line_dim)
        dims_list = [1, 1, 1, 1]
        dims_list[line_dim] = block_len
        right_side = right_side + weights[offset].reshape(dims_list) * shifted
    return right_side


def local_chain(factor, values, axis_pos, reverse):
    pieces = factor.shape[0]
    dims_list = [1] * values.ndim
    dims_list[axis_pos] = pieces
    factors = jnp.broadcast_to(factor.reshape(dims_list), values.shape)
    _, inclusive = lax.associative_scan(compose, (factors, values), reverse=reverse, axis=axis_pos)
    empty = jnp.zeros_like(lax.slice_in_dim(values, 0, 1, axis=axis_pos))
    if reverse:
        return jnp.concatenate(
            [lax.slice_in_dim(inclusive, 1, pieces, axis=axis_pos), empty], axis=axis_pos
        )
    return jnp.concatenate(
        [empty, lax.slice_in_dim(inclusive, 0, pieces - 1, axis=axis_pos)], axis=axis_pos
    )


def wall_whole_lines(line_data):
    pieces = lax.axis_size("wall")
    fields, planes, length_all, columns = line_data.shape
    block_len = length_all // pieces
    weights, down_maps, enter_gain, back_maps, leave_gain = block_tables(pieces, block_len)
    padded = jnp.pad(line_data, ((0, 0), (0, 0), (2, 2), (0, 0)))
    right_side = stencil(padded, weights, length_all, 2)
    blocked = right_side.reshape(fields, planes, pieces, block_len, columns)
    local_part = jnp.einsum("kij,fqkjs->fqkis", down_maps, blocked, precision=HIGHEST_MODE)
    inflow = local_chain(enter_gain[:, -1], local_part[:, :, :, -1, :], 2, False)
    reduced = local_part + enter_gain[None, None, :, :, None] * inflow[:, :, :, None, :]
    swept = jnp.einsum("kij,fqkjs->fqkis", back_maps, reduced, precision=HIGHEST_MODE)
    outflow = local_chain(leave_gain[:, 0], swept[:, :, :, 0, :], 2, True)
    slopes = swept + leave_gain[None, None, :, :, None] * outflow[:, :, :, None, :]
    slopes = slopes.reshape(fields, planes, length_all, columns)
    return lax.all_to_all(slopes, "wall", split_axis=2, concat_axis=1, tiled=True)


def span_whole_lines(line_data):
    pieces = lax.axis_size("span")
    fields, planes, rows_here, length_all = line_data.shape
    block_len = length_all // pieces
    weights, down_maps, enter_gain, back_maps, leave_gain = block_tables(pieces, block_len)
    padded = jnp.pad(line_data, ((0, 0), (0, 0), (0, 0), (2, 2)))
    right_side = stencil(padded, weights, length_all, 3)
    blocked = right_side.reshape(fields, planes, rows_here, pieces, block_len)
    local_part = jnp.einsum("kij,fqwkj->fqwki", down_maps, blocked, precision=HIGHEST_MODE)
    inflow = local_chain(enter_gain[:, -1], local_part[:, :, :, :, -1], 3, False)
    reduced = local_part + enter_gain[None, None, None, :, :] * inflow[:, :, :, :, None]
    swept = jnp.einsum("kij,fqwkj->fqwki", back_maps, reduced, precision=HIGHEST_MODE)
    outflow = local_chain(leave_gain[:, 0], swept[:, :, :, :, 0], 3, True)
    slopes = swept + leave_gain[None, None, None, :, :] * outflow[:, :, :, :, None]
    slopes = slopes.reshape(fields, planes, rows_here, length_all)
    return lax.all_to_all(slopes, "span", split_axis=3, concat_axis=1, tiled=True)


def per_device(conserved, wall_metric, span_metric):
    wall_part = wall_whole_lines(
        lax.all_to_all(conserved, "wall", split_axis=1, concat_axis=2, tiled=True)
    )
    span_part = span_whole_lines(
        lax.all_to_all(conserved, "span", split_axis=1, concat_axis=3, tiled=True)
    )
    return (wall_metric[None] * wall_part, span_metric[None] * span_part)


def solution(mesh):
    in_specs = (
        P(None, "stream", "wall", "span"),
        P("stream", "wall", "span"),
        P("stream", "wall", "span"),
    )
    out_specs = (P(None, "stream", "wall", "span"), P(None, "stream", "wall", "span"))
    return jax.shard_map(
        per_device, mesh=mesh, in_specs=in_specs, out_specs=out_specs, check_vma=False
    )
```

profile of v0, /device:TPU:0, one launch (start us, length us, event | category | flops | bytes accessed | tf_op | source)
XLA Modules:
  0.0 310.7 jit_solution(16295281881544152152)
XLA Ops:
  4.9 50.1 %all_to_all.72 = f32[5,16,96,128]{3,2,0,1:T(8,128)} all-to-all(f32[5,16,96,128]{3,2,0,1:T(8,128)S(1)} %copy.41), channel_id=1, replica_groups=mesh['wall'=4,'span'=4,'stream'=2] {'span'}, dimensions={1} | all-to-all | bytes 7864320 | tf_op jit(solution)/shard_map/all_to_all | solution.py:141
  55.0 5.1 %all-to-all-start = ((f32[5,16,96,128]{3,2,0,1:T(8,128)}), f32[5,16,96,128]{3,2,0,1:T(8,128)}, u32[]{:S(2)}, u32[]{:S(2)}) async-start(f32[5,16,96,128]{3,2,0,1:T(8,128)} %copy-done), calls=%async_computation | async-start | bytes 7864320 | tf_op jit(solution)/shard_map/all_to_all | solution.py:138
  60.5 6.9 %copy.87 = f32[5,4,4,96,128]{4,1,3,2,0:T(4,128)} copy(f32[5,4,4,96,128]{4,3,0,2,1:T(8,128)} %bitcast.70) | data formatting | bytes 7864320 | tf_op jit(solution)/shard_map/all_to_all | solution.py:141
  67.5 5.3 %all_to_all.63 = f32[5,4,96,512]{3,2,1,0:T(8,128)} reshape(f32[5,4,96,4,128]{4,3,2,1,0:T(4,128)} %bitcast.73) | data formatting | bytes 7864320 | tf_op jit(solution)/shard_map/all_to_all | solution.py:141
  72.9 11.5 %fusion.27 = f32[5,4,96,4,128]{4,2,1,0,3:T(8,128)S(1)} fusion(f32[4,128,128,1,1]{2,1,4,3,0:T(8,128)S(1)} %copy-done.23, f32[5,4,96,512]{3,2,1,0:T(8,128)} %all_to_all.63, f32[512]{0:T(512)S(1)} %copy-done.24, f32[512]{0:T(512)S(1)} %copy-done.25, f32[512]{0:T(512)S(1)} %copy-done.26, f32[512]{0:T(512)S(1)} %copy-done.27, f32[512]{0:T(512)S(1)} %copy-done.28), kind=kOutput, calls=%fused_computation.33 | convolution fusion | flops 1518796800 | bytes 8136704 | tf_op jit(solution)/shard_map/kij,fqwkj->fqwki/dot_general | solution.py:126
  86.3 3.0 slice.424
  89.3 2.8 copy.53
  93.2 6.8 %fusion.21 = f32[5,4,96,4,128]{4,2,1,0,3:T(8,128)} fusion(f32[4,128,128,1,1]{2,1,4,3,0:T(8,128)S(1)} %copy-done.7, f32[5,4,96,4,128]{4,2,1,0,3:T(8,128)} %copy-done.3, f32[5,4,96,4]{2,1,0,3:T(4,128)S(1)} %concatenate.29.clone, f32[4,128]{1,0:T(4,128)S(1)} %copy-done.20), kind=kOutput, calls=%fused_computation.31 | convolution fusion | flops 1511915520 | bytes 8159232 | tf_op jit(solution)/shard_map/kij,fqwkj->fqwki/dot_general | solution.py:129
  100.0 2.8 copy.55
  104.0 4.2 %multiply_add_fusion = f32[5,4,96,4,128]{4,2,1,0,3:T(8,128)} fusion(f32[5,4,96,4,128]{4,2,1,0,3:T(8,128)} %fusion.21, f32[5,4,96,4]{2,1,0,3:T(4,128)S(1)} %concatenate.31.clone, f32[4,128]{1,0:T(4,128)S(1)} %copy-done.16), kind=kLoop, calls=%fused_computation.20 | loop fusion | flops 1966080 | bytes 7897088 | tf_op jit(solution)/shard_map/add | solution.py:131
  108.3 6.6 %copy.66 = f32[5,4,96,4,128]{2,1,0,4,3:T(4,128)} copy(f32[5,4,96,4,128]{4,2,1,0,3:T(8,128)} %multiply_add_fusion) | data formatting | bytes 7864320 | tf_op jit(solution)/shard_map/reshape | solution.py:132
  114.9 31.4 %all-to-all-done = f32[5,16,96,128]{3,2,0,1:T(8,128)} async-done(((f32[5,16,96,128]{3,2,0,1:T(8,128)}), f32[5,16,96,128]{3,2,0,1:T(8,128)}, u32[]{:S(2)}, u32[]{:S(2)}) %all-to-all-start) | async-done | bytes 3932192 | tf_op jit(solution)/shard_map/all_to_all | solution.py:138
  146.3 5.1 %all-to-all-start.3 = ((f32[5,4,96,512]{2,1,0,3:T(4,128)}), f32[5,4,96,512]{2,1,0,3:T(4,128)}, u32[]{:S(2)}, u32[]{:S(2)}) async-start(f32[5,4,96,512]{2,1,0,3:T(4,128)} %bitcast.67), calls=%async_computation.3 | async-start | bytes 10485760 | tf_op jit(solution)/shard_map/all_to_all | solution.py:133
  154.0 3.2 %multiply_add_fusion.2 = f32[5,4,384,128]{3,2,1,0:T(8,128)S(1)} fusion(f32[5,4,384,128]{3,2,1,0:T(8,128)S(1)} %bitcast.69, f32[384]{0:T(512)S(1)} %copy-done.11, f32[384]{0:T(512)S(1)} %copy-done.12, f32[384]{0:T(512)S(1)} %copy-done.13, f32[384]{0:T(512)S(1)} %copy-done.14, f32[384]{0:T(512)S(1)} %copy-done.15), kind=kLoop, calls=%fused_computation.28 | loop fusion | flops 8847360 | bytes 7872000 | tf_op jit(solution)/shard_map/add | solution.py:80
  157.2 3.7 %fusion.24 = f32[5,4,4,96,128]{4,3,1,0,2:T(8,128)S(1)} fusion(f32[4,96,96,1,1]{2,1,4,3,0:T(8,128)S(1)} %copy-done.8, f32[5,4,4,96,128]{4,3,2,1,0:T(8,128)S(1)} %bitcast.68), kind=kOutput, calls=%fused_computation.32 | convolution fusion | flops 1132462080 | bytes 8011776 | tf_op jit(solution)/shard_map/kij,fqkjs->fqkis/dot_general | solution.py:108
  163.5 6.4 %fusion.17 = f32[4,5,4,128,96]{3,4,2,1,0:T(8,128)S(1)} fusion(f32[4,96,96,1,1]{2,1,4,3,0:T(8,128)S(1)} %copy-done.9, f32[5,4,4,96,128]{4,3,1,0,2:T(8,128)} %copy-done.2, f32[5,4,4,128]{3,1,0,2:T(4,128)S(1)} %concatenate.25, f32[4,96]{1,0:T(4,128)S(1)} %copy-done.19), kind=kOutput, calls=%fused_computation.25 | convolution fusion | flops 1134428160 | bytes 8054272 | tf_op jit(solution)/shard_map/kij,fqkjs->fqkis/dot_general | solution.py:111
  172.9 6.0 %multiply_add_fusion.1 = f32[5,4,4,96,128]{4,1,0,2,3:T(4,128)S(1)} fusion(f32[5,4,4,128]{3,1,0,2:T(4,128)S(1)} %concatenate.27, f32[4,96]{0,1:T(8,128)S(1)} %copy-done.10, f32[4,5,4,128,96]{3,4,2,1,0:T(8,128)} %copy-done.1), kind=kLoop, calls=%fused_computation.24 | loop fusion | flops 1966080 | bytes 7906816 | tf_op jit(solution)/shard_map/add | solution.py:113
  180.1 4.5 %copy.47 = f32[5,4,384,128]{3,1,0,2:T(4,128)} copy(f32[5,4,384,128]{3,2,1,0:T(8,128)S(1)} %bitcast.74) | data formatting | bytes 7864320 | tf_op jit(solution)/shard_map/reshape | solution.py:114
  184.6 24.9 %all-to-all-done.3 = f32[5,4,96,512]{2,1,0,3:T(4,128)} async-done(((f32[5,4,96,512]{2,1,0,3:T(4,128)}), f32[5,4,96,512]{2,1,0,3:T(4,128)}, u32[]{:S(2)}, u32[]{:S(2)}) %all-to-all-start.3) | async-done | bytes 3932192 | tf_op jit(solution)/shard_map/all_to_all | solution.py:133
  209.5 4.8 %all-to-all-start.1 = ((f32[5,4,384,128]{3,1,0,2:T(4,128)}), f32[5,4,384,128]{3,1,0,2:T(4,128)}, u32[]{:S(2)}, u32[]{:S(2)}) async-start(f32[5,4,384,128]{3,1,0,2:T(4,128)} %copy.47), calls=%async_computation.1 | async-start | bytes 7864320 | tf_op jit(solution)/shard_map/all_to_all | solution.py:115
  214.3 6.7 %copy.60 = f32[5,4,4,96,128]{4,3,2,1,0:T(8,128)} copy(f32[5,4,4,96,128]{3,2,0,4,1:T(4,128)} %bitcast.30) | data formatting | bytes 7864320 | tf_op jit(solution)/shard_map/all_to_all | solution.py:133
  221.0 80.3 %all-to-all-done.1 = f32[5,4,384,128]{3,1,0,2:T(4,128)} async-done(((f32[5,4,384,128]{3,1,0,2:T(4,128)}), f32[5,4,384,128]{3,1,0,2:T(4,128)}, u32[]{:S(2)}, u32[]{:S(2)}) %all-to-all-start.1) | async-done | bytes 3932192 | tf_op jit(solution)/shard_map/all_to_all | solution.py:115
  301.3 2.6 copy.48
  306.5 4.2 %broadcast_multiply_fusion = (f32[5,16,96,128]{3,2,1,0:T(8,128)}, f32[5,16,96,128]{3,2,1,0:T(8,128)}) fusion(f32[5,16,96,128]{3,2,1,0:T(8,128)S(1)} %bitcast.71, f32[16,96,128]{2,1,0:T(8,128)S(1)} %copy-done.5, f32[5,16,96,128]{3,2,1,0:T(8,128)S(1)} %bitcast.72, f32[16,96,128]{2,1,0:T(8,128)S(1)} %copy-done.6), kind=kLoop, calls=%fused_computation.36 | loop fusion | flops 1966080 | bytes 17301504 | tf_op jit(solution)/shard_map/mul | solution.py:143
  (120 shorter events, 20.5 us)
Async XLA Ops:
  55.0 5.1 %copy-start.21 = (f32[2]{0:T(128)S(1)}, f32[2]{0:T(128)}, u32[]{:S(2)}) copy-start(f32[2]{0:T(128)} %constant.103) | copy-start | bytes 28
  55.0 5.2 %copy-start.22 = (f32[2]{0:T(128)S(1)}, f32[2]{0:T(128)}, u32[]{:S(2)}) copy-start(f32[2]{0:T(128)} %constant.128) | copy-start | bytes 28
  55.0 5.3 %copy-start.17 = (f32[2]{0:T(128)S(1)}, f32[2]{0:T(128)}, u32[]{:S(2)}) copy-start(f32[2]{0:T(128)} %constant.94) | copy-start | bytes 28
  55.0 5.4 %copy-start.18 = (f32[2]{0:T(128)S(1)}, f32[2]{0:T(128)}, u32[]{:S(2)}) copy-start(f32[2]{0:T(128)} %constant.119) | copy-start | bytes 28
  55.0 91.4 %all-to-all-start = ((f32[5,16,96,128]{3,2,0,1:T(8,128)}), f32[5,16,96,128]{3,2,0,1:T(8,128)}, u32[]{:S(2)}, u32[]{:S(2)}) async-start(f32[5,16,96,128]{3,2,0,1:T(8,128)} %copy-done), calls=%async_computation | async-start | bytes 7864320 | tf_op jit(solution)/shard_map/all_to_all | solution.py:138
  67.5 5.4 %copy-start.23 = (f32[4,128,128,1,1]{2,1,4,3,0:T(8,128)S(1)}, f32[4,128,128,1,1]{2,1,4,3,0:T(8,128)}, u32[]{:S(2)}) copy-start(f32[4,128,128,1,1]{2,1,4,3,0:T(8,128)} %constant.132) | copy-start | bytes 786436
  67.5 5.4 %copy-start.24 = (f32[512]{0:T(512)S(1)}, f32[512]{0:T(512)}, u32[]{:S(2)}) copy-start(f32[512]{0:T(512)} %constant.114) | copy-start | bytes 6148
  67.5 5.4 %copy-start.25 = (f32[512]{0:T(512)S(1)}, f32[512]{0:T(512)}, u32[]{:S(2)}) copy-start(f32[512]{0:T(512)} %constant.112) | copy-start | bytes 6148
  67.5 5.4 %copy-start.26 = (f32[512]{0:T(512)S(1)}, f32[512]{0:T(512)}, u32[]{:S(2)}) copy-start(f32[512]{0:T(512)} %constant.110) | copy-start | bytes 6148
  67.5 5.4 %copy-start.27 = (f32[512]{0:T(512)S(1)}, f32[512]{0:T(512)}, u32[]{:S(2)}) copy-start(f32[512]{0:T(512)} %constant.108) | copy-start | bytes 6148
  67.5 5.4 %copy-start.28 = (f32[512]{0:T(512)S(1)}, f32[512]{0:T(512)}, u32[]{:S(2)}) copy-start(f32[512]{0:T(512)} %constant.106) | copy-start | bytes 6148
  89.3 3.9 %copy-start.7 = (f32[4,128,128,1,1]{2,1,4,3,0:T(8,128)S(1)}, f32[4,128,128,1,1]{2,1,4,3,0:T(8,128)}, u32[]{:S(2)}) copy-start(f32[4,128,128,1,1]{2,1,4,3,0:T(8,128)} %constant.133) | copy-start | bytes 786436
  89.3 3.9 %copy-start.20 = (f32[4,128]{1,0:T(4,128)S(1)}, f32[4,128]{1,0:T(4,128)}, u32[]{:S(2)}) copy-start(f32[4,128]{1,0:T(4,128)} %constant.33.clone) | copy-start | bytes 6148
  100.0 4.0 %copy-start.16 = (f32[4,128]{1,0:T(4,128)S(1)}, f32[4,128]{1,0:T(4,128)}, u32[]{:S(2)}) copy-start(f32[4,128]{1,0:T(4,128)} %constant.35.clone) | copy-start | bytes 6148
  146.3 63.1 %all-to-all-start.3 = ((f32[5,4,96,512]{2,1,0,3:T(4,128)}), f32[5,4,96,512]{2,1,0,3:T(4,128)}, u32[]{:S(2)}, u32[]{:S(2)}) async-start(f32[5,4,96,512]{2,1,0,3:T(4,128)} %bitcast.67), calls=%async_computation.3 | async-start | bytes 10485760 | tf_op jit(solution)/shard_map/all_to_all | solution.py:133
  151.4 2.5 copy-start.11
  151.4 2.5 copy-start.12
  153.9 3.2 %copy-start.8 = (f32[4,96,96,1,1]{2,1,4,3,0:T(8,128)S(1)}, f32[4,96,96,1,1]{2,1,4,3,0:T(8,128)}, u32[]{:S(2)}) copy-start(f32[4,96,96,1,1]{2,1,4,3,0:T(8,128)} %constant.130) | copy-start | bytes 442372
  157.2 6.3 %copy-start.9 = (f32[4,96,96,1,1]{2,1,4,3,0:T(8,128)S(1)}, f32[4,96,96,1,1]{2,1,4,3,0:T(8,128)}, u32[]{:S(2)}) copy-start(f32[4,96,96,1,1]{2,1,4,3,0:T(8,128)} %constant.131) | copy-start | bytes 442372
  157.2 6.3 %copy-start.19 = (f32[4,96]{1,0:T(4,128)S(1)}, f32[4,96]{1,0:T(4,128)}, u32[]{:S(2)}) copy-start(f32[4,96]{1,0:T(4,128)} %constant.28.clone) | copy-start | bytes 4612
  169.9 2.6 copy-start.1
  169.9 3.0 copy-start.10
  209.5 91.9 %all-to-all-start.1 = ((f32[5,4,384,128]{3,1,0,2:T(4,128)}), f32[5,4,384,128]{3,1,0,2:T(4,128)}, u32[]{:S(2)}, u32[]{:S(2)}) async-start(f32[5,4,384,128]{3,1,0,2:T(4,128)} %copy.47), calls=%async_computation.1 | async-start | bytes 7864320 | tf_op jit(solution)/shard_map/all_to_all | solution.py:115
  303.9 2.5 copy-start.6
  (8 other events, 17.5 us)
where the time goes:
time: 312 us; the launch traced here: 311 us
  waiting for transfers between devices  137 us (44%)
  local copies, waits for them, and re-layouts  61.2 us (20%)
  blocking collectives  50.1 us (16%)
  matrix products  28.3 us (9%)
  other arithmetic  18.2 us (6%)
  starting transfers between devices  15 us (5%)
    all_to_all x1, waiting for transfers between devices, wall_whole_lines(): lax.all_to_all(slopes, 'wall', split_axis=2, concat_axis=1, tiled=True)  80.3 us
    all_to_all x1, blocking collectives, per_device(): lax.all_to_all(conserved, 'span', split_axis=1, concat_axis=3, tiled=True)  50.1 us
    all_to_all x1, waiting for transfers between devices, per_device(): lax.all_to_all(conserved, 'wall', split_axis=1, concat_axis=2, tiled=True)  31.4 us
    all_to_all x1, waiting for transfers between devices, span_whole_lines(): lax.all_to_all(slopes, 'span', split_axis=3, concat_axis=1, tiled=True)  24.9 us
    all_to_all x2, local copies, waits for them, and re-layouts, per_device(): lax.all_to_all(conserved, 'span', split_axis=1, concat_axis=3, tiled=True)  12.3 us
    dot_general x1, matrix products, span_whole_lines(): jnp.einsum('kij,fqwkj->fqwki', down_maps, blocked, precision=HIGHEST_MODE)  11.5 us
    unnamed x65, local copies, waits for them, and re-layouts  11.4 us
    dot_general x1, matrix products, span_whole_lines(): jnp.einsum('kij,fqwkj->fqwki', back_maps, reduced, precision=HIGHEST_MODE)  6.78 us
  transfers between devices with their start and end apart: 3, of which 3 were waited for; matrix products, arithmetic and copies ran while one was open for 27% of the time, Pallas kernels for 0%

commit v1 on v0

v1 whole, which is shorter than its diff:
```python
import functools

import jax
import jax.numpy as jnp
import ml_dtypes
import numpy as np
from jax import lax
from jax.experimental import pallas as pl
from jax.experimental.pallas import tpu as pltpu
from jax.sharding import PartitionSpec as P

band_alpha = 0.4995
MESH = pl.DeviceIdType.MESH


def line_operators(length_all):
    lower_band = np.full(length_all, band_alpha)
    lower_band[[1, length_all - 2]] = 0.25
    lower_band[[0, length_all - 1]] = 0.0
    band = np.eye(length_all)
    rows = np.arange(length_all)
    band[rows[1:], rows[:-1]] = lower_band[1:]
    band[rows[:-1], rows[1:]] = lower_band[:-1]
    near_coef = (band_alpha + 2.0) / 3.0
    far_coef = (4.0 * band_alpha - 1.0) / 12.0
    weights = np.zeros((5, length_all))
    weights[:, :] = np.array([-far_coef, -near_coef, 0.0, near_coef, far_coef])[:, None]
    weights[:, 1] = [0.0, -0.75, 0.0, 0.75, 0.0]
    weights[:, length_all - 2] = [0.0, -0.75, 0.0, 0.75, 0.0]
    weights[:, 0] = [0.0, 0.0, -1.5, 2.0, -0.5]
    weights[:, length_all - 1] = [0.5, -2.0, 1.5, 0.0, 0.0]
    right = np.zeros((length_all, length_all))
    for offset in range(-2, 3):
        good = rows[(rows + offset >= 0) & (rows + offset < length_all)]
        right[good, good + offset] = weights[offset + 2, good]
    inverse = np.linalg.inv(band)
    return inverse, inverse @ right


def block_tables(pieces, block):
    inverse, whole = line_operators(pieces * block)
    own = np.zeros((pieces, block, block))
    fix = np.zeros((pieces, block, 8))
    sends = np.zeros((pieces, 8, block))
    gains = np.zeros((2, pieces, max(pieces - 1, 1)))
    half = block // 2
    for p in range(pieces):
        lo, hi = p * block, (p + 1) * block
        own[p] = whole[lo:hi, lo:hi]
        sends[p, 1, block - 2] = sends[p, 2, block - 1] = 1.0
        sends[p, 4, 0] = sends[p, 5, 1] = 1.0
        if p + 1 < pieces:
            shape = inverse[hi : hi + block, hi - 1] / inverse[hi, hi - 1]
            sends[p, 0] = whole[hi + half, lo:hi] / shape[half]
            fix[p + 1, :, 0] = shape
            near = whole[hi : hi + block, hi - 2 : hi]
            fix[p + 1, :, 1:3] = near - shape[:, None] * sends[p, 0, block - 2 :]
            for d in range(1, pieces - p):
                gains[0, p + d, d - 1] = inverse[lo + d * block, hi - 1] / inverse[hi, hi - 1]
        if p > 0:
            shape = inverse[lo - block : lo, lo] / inverse[lo - 1, lo]
            sends[p, 3] = whole[lo - block + half, lo:hi] / shape[half]
            fix[p - 1, :, 3] = shape
            near = whole[lo - block : lo, lo : lo + 2]
            fix[p - 1, :, 4:6] = near - shape[:, None] * sends[p, 3, :2]
            for d in range(1, p + 1):
                gains[1, p - d, d - 1] = inverse[hi - 1 - d * block, lo] / inverse[lo - 1, lo]
    return own, fix, sends, gains


def split(table):
    high = table.astype(ml_dtypes.bfloat16)
    low = (table - high.astype(np.float64)).astype(ml_dtypes.bfloat16)
    return high, low


def halves(values):
    high = values.astype(jnp.bfloat16)
    low = (values - high.astype(jnp.float32)).astype(jnp.bfloat16)
    return high, low


def exchange_kernel(
    wall_n, span_n,
    f_hbm, wall_sends, span_sends, gains, wall_tab, span_tab, span_fix,
    wall_msg, span_msg, wall_mine, span_mine, fix_mine,
    f_buf, wall_v, span_v, wall_out, span_out, wall_near, span_near, wall_far, span_far,
    load_sems, table_sems, send_sems, recv_sems,
):
    me_w, me_s, me_c = (lax.axis_index(name) for name in ("wall", "span", "stream"))
    fields, planes, rows, columns = f_buf.shape
    loads = [pltpu.make_async_copy(f_hbm.at[k], f_buf.at[k], load_sems.at[k]) for k in range(fields)]
    tables = [
        pltpu.make_async_copy(src, dst, table_sems.at[k])
        for k, (src, dst) in enumerate((
            (wall_sends.at[me_w], wall_v), (span_sends.at[me_s], span_v),
            (wall_tab.at[me_w], wall_mine), (span_tab.at[me_s], span_mine),
            (span_fix.at[me_s], fix_mine),
        ))
    ]
    for copy in tables[:2] + loads + tables[2:]:
        copy.start()

    def device(axis, shift):
        if axis == 0:
            return (me_w + shift, me_s, me_c)
        return (me_w, me_s + shift, me_c)

    axes = ((0, me_w, wall_n), (1, me_s, span_n))
    barrier = pltpu.get_barrier_semaphore()
    for axis, me, n in axes:
        for d in range(1, n):
            @pl.when(me + d < n)
            def _():
                pl.semaphore_signal(barrier, inc=1, device_id=device(axis, d), device_id_type=MESH)

            @pl.when(me >= d)
            def _():
                pl.semaphore_signal(barrier, inc=1, device_id=device(axis, -d), device_id_type=MESH)

    wall_msg[...] = jnp.zeros_like(wall_msg)
    span_msg[...] = jnp.zeros_like(span_msg)
    outs, nears, fars = (wall_out, span_out), (wall_near, span_near), (wall_far, span_far)

    def transfer(axis, side, d):
        if d == 1:
            src, dst = outs[axis].at[pl.ds(3 * side, 3)], nears[axis].at[side]
        else:
            src, dst = outs[axis].at[3 * side], fars[axis].at[side, d - 2]
        return pltpu.make_async_remote_copy(
            src_ref=src, dst_ref=dst,
            send_sem=send_sems.at[axis, side, d - 1], recv_sem=recv_sems.at[axis, side, d - 1],
            device_id=device(axis, d if side == 0 else -d), device_id_type=MESH,
        )

    def has_target(me, n, side, d):
        return me + d < n if side == 0 else me >= d

    def has_source(me, n, side, d):
        return me >= d if side == 0 else me + d < n

    def send_all(axis, me, n):
        for d in range(n - 1, 0, -1):
            for side in range(2):
                @pl.when(has_target(me, n, side, d))
                def _():
                    transfer(axis, side, d).start()

    tables[0].wait()
    for k in range(fields):
        loads[k].wait()
        here = pl.ds(k * planes, planes)
        values = f_buf[k]
        wall_out[0, here, :] = jnp.sum(values * wall_v[0][None], axis=1)
        wall_out[3, here, :] = jnp.sum(values * wall_v[1][None], axis=1)
        wall_out[1, here, :] = f_buf[k, :, rows - 2, :]
        wall_out[2, here, :] = f_buf[k, :, rows - 1, :]
        wall_out[4, here, :] = f_buf[k, :, 0, :]
        wall_out[5, here, :] = f_buf[k, :, 1, :]
    pl.semaphore_wait(barrier, wall_n + span_n - 2)
    send_all(*axes[0])

    tables[1].wait()
    tiles = planes * rows // 128
    for k in range(fields):
        high, low = halves(f_buf[k].reshape(planes * rows, columns))
        both = jnp.concatenate([high, low], axis=1)
        picked = lax.dot_general(
            span_v[...], both, (((1,), (1,)), ((), ())), preferred_element_type=jnp.float32
        )
        picked = picked[:8] + picked[8:]
        for t in range(tiles):
            for m in range(6):
                span_out[m, k * tiles + t : k * tiles + t + 1, :] = picked[m : m + 1, t * 128 : (t + 1) * 128]
    send_all(*axes[1])

    msgs = (wall_msg, span_msg)
    for axis, me, n in axes:
        for d in range(1, n):
            for side in range(2):
                @pl.when(has_source(me, n, side, d))
                def _():
                    transfer(axis, side, d).wait_recv()
                    gain = gains[axis, side, me, d - 1]
                    if d == 1:
                        msgs[axis][3 * side] += gain * nears[axis][side, 0]
                        msgs[axis][3 * side + 1] = nears[axis][side, 1]
                        msgs[axis][3 * side + 2] = nears[axis][side, 2]
                    else:
                        msgs[axis][3 * side] += gain * fars[axis][side, d - 2]
    for axis, me, n in axes:
        for d in range(1, n):
            for side in range(2):
                @pl.when(has_target(me, n, side, d))
                def _():
                    transfer(axis, side, d).wait_send()
    for copy in tables[2:]:
        copy.wait()


def slope_kernel(f_ref, wall_metric, span_metric, wall_msg, span_msg, wall_tab, span_tab, fix_tab, wall_ref, span_ref):
    fields, planes, rows, columns = f_ref.shape
    step = pl.program_id(0)
    steps = pl.num_programs(0)
    tiles = planes * rows // 128
    for k in range(fields):
        high, low = halves(f_ref[k])
        both = jnp.concatenate([high, low], axis=2).reshape(planes * rows, 2 * columns)
        spread = jnp.dot(both, span_tab[...], preferred_element_type=jnp.float32)
        first = (k * steps + step) * tiles
        edge = jnp.concatenate([span_msg[:, first + t, :] for t in range(tiles)], axis=1)
        edge_high, edge_low = halves(edge)
        edges = jnp.concatenate([edge_high.astype(jnp.float32), edge_low.astype(jnp.float32)], axis=0).T
        spread += jnp.dot(edges.astype(jnp.bfloat16), fix_tab[...], preferred_element_type=jnp.float32)
        spread = spread[:, :columns] + spread[:, columns:]
        span_ref[k] = spread.reshape(planes, rows, columns) * span_metric[...]
        for q in range(0, planes, 2):
            parts = []
            for j in (q, q + 1):
                msg_high, msg_low = halves(wall_msg[:, (k * steps + step) * planes + j, :])
                parts.append(jnp.concatenate(
                    [high[j], low[j], jnp.concatenate([msg_high, msg_low], axis=0)], axis=0
                ))
            pair = jnp.concatenate(parts, axis=1)
            solved = jnp.dot(wall_tab[...], pair, preferred_element_type=jnp.float32)
            solved = solved[:rows] + solved[rows:]
            wall_ref[k, q] = solved[:, :columns] * wall_metric[q]
            wall_ref[k, q + 1] = solved[:, columns:] * wall_metric[q + 1]


def per_device(wall_n, span_n, conserved, wall_metric, span_metric):
    fields, planes, rows, columns = conserved.shape
    slabs = fields * planes
    lines = slabs * rows // 128
    own_w, fix_w, sends_w, gains_w = block_tables(wall_n, rows)
    own_s, fix_s, sends_s, gains_s = block_tables(span_n, columns)
    bf16 = jnp.bfloat16

    wall_sends = np.broadcast_to(sends_w[:, (0, 3), :, None], (wall_n, 2, rows, 128)).astype(np.float32)
    high, low = split(sends_s)
    span_sends = np.concatenate([np.concatenate([t, t], axis=2) for t in (high, low)], axis=1)
    most = max(wall_n, span_n)
    gains = np.zeros((2, 2, most, most), np.float32)
    gains[0, :, :wall_n, : gains_w.shape[2]] = gains_w
    gains[1, :, :span_n, : gains_s.shape[2]] = gains_s
    own_high, own_low = split(own_w)
    fix_high, fix_low = split(fix_w)
    wall_tab = np.concatenate([
        np.concatenate([own_high, own_high, fix_high, fix_high], axis=2),
        np.concatenate([own_low, own_low, fix_low, fix_low], axis=2),
    ], axis=1)
    own_high, own_low = split(own_s.transpose(0, 2, 1))
    span_tab = np.concatenate([np.concatenate([own_high, own_low], axis=2)] * 2, axis=1)
    fix_high, fix_low = split(fix_s.transpose(0, 2, 1))
    span_fix = np.concatenate([np.concatenate([fix_high, fix_low], axis=2)] * 2, axis=1)

    vmem = pl.BlockSpec(memory_space=pltpu.VMEM)
    anywhere = pl.BlockSpec(memory_space=pl.ANY)
    far = max(wall_n, span_n) - 1
    wall_msg, span_msg, wall_mine, span_mine, fix_mine = pl.pallas_call(
        functools.partial(exchange_kernel, wall_n, span_n),
        out_shape=(
            jax.ShapeDtypeStruct((8, slabs, 128), jnp.float32),
            jax.ShapeDtypeStruct((8, lines, 128), jnp.float32),
            jax.ShapeDtypeStruct(wall_tab.shape[1:], bf16),
            jax.ShapeDtypeStruct(span_tab.shape[1:], bf16),
            jax.ShapeDtypeStruct(span_fix.shape[1:], bf16),
        ),
        in_specs=[anywhere, anywhere, anywhere, pl.BlockSpec(memory_space=pltpu.SMEM), anywhere, anywhere, anywhere],
        out_specs=(vmem, vmem, anywhere, anywhere, anywhere),
        scratch_shapes=[
            pltpu.VMEM(conserved.shape, jnp.float32),
            pltpu.VMEM(wall_sends.shape[1:], jnp.float32),
            pltpu.VMEM(span_sends.shape[1:], bf16),
            pltpu.VMEM((6, slabs, 128), jnp.float32),
            pltpu.VMEM((6, lines, 128), jnp.float32),
            pltpu.VMEM((2, 3, slabs, 128), jnp.float32),
            pltpu.VMEM((2, 3, lines, 128), jnp.float32),
            pltpu.VMEM((2, max(wall_n - 2, 1), slabs, 128), jnp.float32),
            pltpu.VMEM((2, max(span_n - 2, 1), lines, 128), jnp.float32),
            pltpu.SemaphoreType.DMA((fields,)),
            pltpu.SemaphoreType.DMA((5,)),
            pltpu.SemaphoreType.DMA((2, 2, far)),
            pltpu.SemaphoreType.DMA((2, 2, far)),
        ],
        compiler_params=pltpu.CompilerParams(
            collective_id=0, has_side_effects=True, vmem_limit_bytes=40 * 1024 * 1024
        ),
        name="exchange",
    )(
        conserved, jnp.asarray(wall_sends), jnp.asarray(span_sends), jnp.asarray(gains),
        jnp.asarray(wall_tab), jnp.asarray(span_tab), jnp.asarray(span_fix),
    )

    step_planes = 4
    steps = planes // step_planes
    fields_block = pl.BlockSpec((fields, step_planes, rows, columns), lambda i: (0, i, 0, 0))
    metric_block = pl.BlockSpec((step_planes, rows, columns), lambda i: (i, 0, 0))
    whole = lambda array: pl.BlockSpec(array.shape, lambda i: (0,) * array.ndim)
    flops = 2 * slabs * (rows * 256 * 256 + 192 * 256 * 128)
    return pl.pallas_call(
        slope_kernel,
        grid=(steps,),
        out_shape=(jax.ShapeDtypeStruct(conserved.shape, jnp.float32),) * 2,
        in_specs=[fields_block, metric_block, metric_block]
        + [whole(t) for t in (wall_msg, span_msg, wall_mine, span_mine, fix_mine)],
        out_specs=(fields_block, fields_block),
        compiler_params=pltpu.CompilerParams(vmem_limit_bytes=40 * 1024 * 1024),
        cost_estimate=pl.CostEstimate(flops=flops, bytes_accessed=17 * conserved.size, transcendentals=0),
        name="slopes",
    )(conserved, wall_metric, span_metric, wall_msg, span_msg, wall_mine, span_mine, fix_mine)


def solution(mesh):
    in_specs = (
        P(None, "stream", "wall", "span"),
        P("stream", "wall", "span"),
        P("stream", "wall", "span"),
    )
    out_specs = (P(None, "stream", "wall", "span"), P(None, "stream", "wall", "span"))
    sizes = (mesh.shape["wall"], mesh.shape["span"])
    return jax.shard_map(
        functools.partial(per_device, *sizes), mesh=mesh, in_specs=in_specs, out_specs=out_specs, check_vma=False
    )
```

time: 312 us -> 28.2 us (0.09)
  waiting for transfers between devices: 137 us -> 0 us
  local copies, waits for them, and re-layouts: 61.2 us -> 7.36 us
  blocking collectives: 50.1 us -> 0 us
  matrix products: 28.3 us -> 0 us
  Pallas kernels: 0 us -> 19.7 us
  other arithmetic: 18.2 us -> 0 us
  starting transfers between devices: 15 us -> 0 us
    all_to_all x3 -> x0, waiting for transfers between devices: 137 us -> none  [the longest x1 80.3 us: wall_whole_lines(): lax.all_to_all(slopes, 'wall', split_axis=2, concat_axis=1, tiled=True)]
    all_to_all x1 -> x0, blocking collectives: 50.1 us -> none  [per_device(): lax.all_to_all(conserved, 'span', split_axis=1, concat_axis=3, tiled=True)]
    dot_general x4 -> x0, matrix products: 28.3 us -> none  [the longest x1 11.5 us: span_whole_lines(): jnp.einsum('kij,fqwkj->fqwki', down_maps, blocked, precision=HIGHEST_MODE)]
    all_to_all x6 -> x0, local copies, waits for them, and re-layouts: 24.3 us -> none  [the longest x2 12.3 us: per_device(): lax.all_to_all(conserved, 'span', split_axis=1, concat_axis=3, tiled=True)]
    pallas_call x0 -> x2, Pallas kernels: none -> 19.7 us  [the longest x1 13.8 us: per_device(): pl.pallas_call(functools.partial(exchange_kernel, wall_n, span_n), out_sh...]
    all_to_all x3 -> x0, starting transfers between devices: 15 us -> none  [the longest x1 5.1 us: per_device(): lax.all_to_all(conserved, 'wall', split_axis=1, concat_axis=2, tiled=True)]
    add x15 -> x0, other arithmetic: 13.7 us -> none  [the longest x1 5.96 us: wall_whole_lines(): swept + leave_gain[None, None, :, :, None] * outflow[:, :, :, None, :]]
    reshape x2 -> x0, local copies, waits for them, and re-layouts: 11.1 us -> none  [the longest x1 6.63 us: span_whole_lines(): slopes = slopes.reshape(fields, planes, rows_here, length_all)]
  transfers between devices with their start and end apart: 3 -> 0, of which waited for: 3 -> 0; matrix products, arithmetic and copies ran while one was open for 27% -> 0% of each run, Pallas kernels for 0% -> 0%
where the time goes in v1:
time: 28.2 us; the launch traced here: 27.8 us
  Pallas kernels  19.7 us (70%)
  local copies, waits for them, and re-layouts  7.36 us (26%)
  between operations  0.67 us (2%)
    pallas_call x1, Pallas kernels, per_device(): pl.pallas_call(functools.partial(exchange_kernel, wall_n, span_n), out_sh...  13.8 us
    unnamed x18, local copies, waits for them, and re-layouts  7.36 us
    pallas_call x1, Pallas kernels, per_device(): pl.pallas_call(slope_kernel, grid=(steps,), out_shape=(jax.ShapeDtypeStru...  5.91 us

profile of v1, /device:TPU:0, one launch (start us, length us, event | category | flops | bytes accessed | tf_op | source)
XLA Modules:
  0.0 27.8 jit_solution(4444949109908103359)
XLA Ops:
  0.6 0.0 copy-start
  0.6 2.1 %copy-done = f32[5,16,96,128]{3,2,1,0:T(8,128)S(1)} copy-done((f32[5,16,96,128]{3,2,1,0:T(8,128)S(1)}, f32[5,16,96,128]{3,2,1,0:T(8,128)}, u32[]{:S(2)}) %copy-start) | copy-done | bytes 3932184
  2.7 0.0 copy-start.1
  2.7 1.0 %copy-done.1 = bf16[4,256,256]{2,1,0:T(8,128)(2,1)S(1)} copy-done((bf16[4,256,256]{2,1,0:T(8,128)(2,1)S(1)}, bf16[4,256,256]{2,1,0:T(8,128)(2,1)}, u32[]{:S(2)}) %copy-start.1) | copy-done | bytes 524312
  3.8 0.0 copy-start.2
  3.8 1.0 %copy-done.2 = bf16[4,192,208]{2,1,0:T(8,128)(2,1)S(1)} copy-done((bf16[4,192,208]{2,1,0:T(8,128)(2,1)S(1)}, bf16[4,192,208]{2,1,0:T(8,128)(2,1)}, u32[]{:S(2)}) %copy-start.2) | copy-done | bytes 319512
  4.8 0.0 copy-start.3
  4.8 1.0 %copy-done.3 = f32[4,2,96,128]{3,2,1,0:T(8,128)S(1)} copy-done((f32[4,2,96,128]{3,2,1,0:T(8,128)S(1)}, f32[4,2,96,128]{3,2,1,0:T(8,128)}, u32[]{:S(2)}) %copy-start.3) | copy-done | bytes 393240
  5.8 0.0 copy-start.4
  5.8 0.8 %copy-done.4 = bf16[4,16,256]{2,1,0:T(8,128)(2,1)S(1)} copy-done((bf16[4,16,256]{2,1,0:T(8,128)(2,1)S(1)}, bf16[4,16,256]{2,1,0:T(8,128)(2,1)}, u32[]{:S(2)}) %copy-start.4) | copy-done | bytes 32792
  6.5 0.0 copy-start.5
  6.5 0.8 %copy-done.5 = bf16[4,16,256]{2,1,0:T(8,128)(2,1)S(1)} copy-done((bf16[4,16,256]{2,1,0:T(8,128)(2,1)S(1)}, bf16[4,16,256]{2,1,0:T(8,128)(2,1)}, u32[]{:S(2)}) %copy-start.5) | copy-done | bytes 32792
  7.3 0.0 copy-start.6
  7.3 0.7 %copy-done.6 = f32[2,2,4,4]{3,2,1,0:T(4,128)S(1)} copy-done((f32[2,2,4,4]{3,2,1,0:T(4,128)S(1)}, f32[2,2,4,4]{3,2,1,0:T(4,128)}, u32[]{:S(2)}) %copy-start.6) | copy-done | bytes 280
  8.0 0.0 copy-start.7
  8.0 0.0 copy-start.8
  8.0 13.8 %exchange.1 = (f32[8,80,128]{2,1,0:T(8,128)S(1)}, f32[8,60,128]{2,1,0:T(8,128)S(1)}, bf16[192,208]{1,0:T(8,128)(2,1)S(1)}, bf16[256,256]{1,0:T(8,128)(2,1)S(1)}, bf16[16,256]{1,0:T(8,128)(2,1)S(1)}) custom-call(f32[5,16,96,128]{3,2,1,0:T(8,128)S(1)} %copy-done, f32[4,2,96,128]{3,2,1,0:T(8,128)S(1)} %copy-done.3, bf16[4,16,256]{2,1,0:T(8,128)(2,1)S(1)} %copy-done.5, ...), custom_call_target="tpu_custom_call" | custom-call | tf_op jit(solution)/shard_map/exchange/pallas_call | solution.py:260
  21.8 0.0 copy-done.7
  21.8 0.0 copy-done.8
  21.8 5.9 %slopes.1 = (f32[5,16,96,128]{3,2,1,0:T(8,128)}, f32[5,16,96,128]{3,2,1,0:T(8,128)}) custom-call(f32[5,16,96,128]{3,2,1,0:T(8,128)S(1)} %copy-done, f32[16,96,128]{2,1,0:T(8,128)S(1)} %copy-done.7, f32[16,96,128]{2,1,0:T(8,128)S(1)} %copy-done.8, f32[8,80,128]{2,1,0:T(8,128)S(1)} %get-tuple-element.7.wall_msg, f32[8,60,128]{2,1,0:T(8,128)S(1)} %get-tuple-element.8.span_msg, ...), custom_call_target="tpu_custom_call" | custom-call | flops 2013265920 | bytes 16711680 | tf_op jit(solution)/shard_map/slopes/pallas_call | solution.py:301
Async XLA Ops:
  0.6 2.1 %copy-start = (f32[5,16,96,128]{3,2,1,0:T(8,128)S(1)}, f32[5,16,96,128]{3,2,1,0:T(8,128)}, u32[]{:S(2)}) copy-start(f32[5,16,96,128]{3,2,1,0:T(8,128)} %f_ref.1) | copy-start | bytes 11796484
  2.7 1.0 %copy-start.1 = (bf16[4,256,256]{2,1,0:T(8,128)(2,1)S(1)}, bf16[4,256,256]{2,1,0:T(8,128)(2,1)}, u32[]{:S(2)}) copy-start(bf16[4,256,256]{2,1,0:T(8,128)(2,1)} %constant.16.clone.span_tab) | copy-start | bytes 1572868
  3.8 1.0 %copy-start.2 = (bf16[4,192,208]{2,1,0:T(8,128)(2,1)S(1)}, bf16[4,192,208]{2,1,0:T(8,128)(2,1)}, u32[]{:S(2)}) copy-start(bf16[4,192,208]{2,1,0:T(8,128)(2,1)} %constant.15.clone.wall_tab) | copy-start | bytes 958468
  4.8 1.0 %copy-start.3 = (f32[4,2,96,128]{3,2,1,0:T(8,128)S(1)}, f32[4,2,96,128]{3,2,1,0:T(8,128)}, u32[]{:S(2)}) copy-start(f32[4,2,96,128]{3,2,1,0:T(8,128)} %constant.12.clone.wall_sends) | copy-start | bytes 1179652
  5.8 0.8 %copy-start.4 = (bf16[4,16,256]{2,1,0:T(8,128)(2,1)S(1)}, bf16[4,16,256]{2,1,0:T(8,128)(2,1)}, u32[]{:S(2)}) copy-start(bf16[4,16,256]{2,1,0:T(8,128)(2,1)} %constant.17.clone.span_fix) | copy-start | bytes 98308
  6.5 0.8 %copy-start.5 = (bf16[4,16,256]{2,1,0:T(8,128)(2,1)S(1)}, bf16[4,16,256]{2,1,0:T(8,128)(2,1)}, u32[]{:S(2)}) copy-start(bf16[4,16,256]{2,1,0:T(8,128)(2,1)} %constant.13.clone.span_sends) | copy-start | bytes 98308
  7.3 0.7 %copy-start.6 = (f32[2,2,4,4]{3,2,1,0:T(4,128)S(1)}, f32[2,2,4,4]{3,2,1,0:T(4,128)}, u32[]{:S(2)}) copy-start(f32[2,2,4,4]{3,2,1,0:T(4,128)} %constant.14.clone.gains) | copy-start | bytes 772
  8.0 13.8 %copy-start.7 = (f32[16,96,128]{2,1,0:T(8,128)S(1)}, f32[16,96,128]{2,1,0:T(8,128)}, u32[]{:S(2)}) copy-start(f32[16,96,128]{2,1,0:T(8,128)} %wall_metric.1) | copy-start | bytes 2359300
  8.0 13.8 %copy-start.8 = (f32[16,96,128]{2,1,0:T(8,128)S(1)}, f32[16,96,128]{2,1,0:T(8,128)}, u32[]{:S(2)}) copy-start(f32[16,96,128]{2,1,0:T(8,128)} %span_metric.1) | copy-start | bytes 2359300

commit v2 on v1

v2 whole, which is shorter than its diff:
```python
import functools

import jax
import jax.numpy as jnp
import ml_dtypes
import numpy as np
from jax import lax
from jax.experimental import pallas as pl
from jax.experimental.pallas import tpu as pltpu
from jax.sharding import PartitionSpec as P

band_alpha = 0.4995
MESH = pl.DeviceIdType.MESH


def line_operators(length_all):
    lower_band = np.full(length_all, band_alpha)
    lower_band[[1, length_all - 2]] = 0.25
    lower_band[[0, length_all - 1]] = 0.0
    band = np.eye(length_all)
    rows = np.arange(length_all)
    band[rows[1:], rows[:-1]] = lower_band[1:]
    band[rows[:-1], rows[1:]] = lower_band[:-1]
    near_coef = (band_alpha + 2.0) / 3.0
    far_coef = (4.0 * band_alpha - 1.0) / 12.0
    weights = np.zeros((5, length_all))
    weights[:, :] = np.array([-far_coef, -near_coef, 0.0, near_coef, far_coef])[:, None]
    weights[:, 1] = [0.0, -0.75, 0.0, 0.75, 0.0]
    weights[:, length_all - 2] = [0.0, -0.75, 0.0, 0.75, 0.0]
    weights[:, 0] = [0.0, 0.0, -1.5, 2.0, -0.5]
    weights[:, length_all - 1] = [0.5, -2.0, 1.5, 0.0, 0.0]
    right = np.zeros((length_all, length_all))
    for offset in range(-2, 3):
        good = rows[(rows + offset >= 0) & (rows + offset < length_all)]
        right[good, good + offset] = weights[offset + 2, good]
    inverse = np.linalg.inv(band)
    return inverse, inverse @ right


def block_tables(pieces, block):
    inverse, whole = line_operators(pieces * block)
    own = np.zeros((pieces, block, block))
    fix = np.zeros((pieces, block, 8))
    sends = np.zeros((pieces, 8, block))
    gains = np.zeros((2, pieces, max(pieces - 1, 1)))
    half = block // 2
    for p in range(pieces):
        lo, hi = p * block, (p + 1) * block
        own[p] = whole[lo:hi, lo:hi]
        sends[p, 1, block - 2] = sends[p, 2, block - 1] = 1.0
        sends[p, 4, 0] = sends[p, 5, 1] = 1.0
        if p + 1 < pieces:
            shape = inverse[hi : hi + block, hi - 1] / inverse[hi, hi - 1]
            sends[p, 0] = whole[hi + half, lo:hi] / shape[half]
            fix[p + 1, :, 0] = shape
            near = whole[hi : hi + block, hi - 2 : hi]
            fix[p + 1, :, 1:3] = near - shape[:, None] * sends[p, 0, block - 2 :]
            for d in range(1, pieces - p):
                gains[0, p + d, d - 1] = inverse[lo + d * block, hi - 1] / inverse[hi, hi - 1]
        if p > 0:
            shape = inverse[lo - block : lo, lo] / inverse[lo - 1, lo]
            sends[p, 3] = whole[lo - block + half, lo:hi] / shape[half]
            fix[p - 1, :, 3] = shape
            near = whole[lo - block : lo, lo : lo + 2]
            fix[p - 1, :, 4:6] = near - shape[:, None] * sends[p, 3, :2]
            for d in range(1, p + 1):
                gains[1, p - d, d - 1] = inverse[hi - 1 - d * block, lo] / inverse[lo - 1, lo]
    return own, fix, sends, gains


def split(table):
    high = table.astype(ml_dtypes.bfloat16)
    low = (table - high.astype(np.float64)).astype(ml_dtypes.bfloat16)
    return high, low


def halves(values):
    high = values.astype(jnp.bfloat16)
    low = (values - high.astype(jnp.float32)).astype(jnp.bfloat16)
    return high, low


def exchange_kernel(
    wall_n, span_n, wall_gains, span_gains,
    f_hbm, wall_tab, span_tab,
    wall_loc, span_loc, wall_msg, span_msg, wall_fix, span_fix,
    f_buf, wall_t, span_t, wall_out, span_out, wall_near, span_near, wall_far, span_far,
    load_sems, table_sems, send_sems, recv_sems,
):
    me_w, me_s, me_c = (lax.axis_index(name) for name in ("wall", "span", "stream"))
    fields, planes, rows, columns = f_hbm.shape
    slabs = fields * planes
    loads = [
        pltpu.make_async_copy(f_hbm.at[k], f_buf.at[pl.ds(k * planes, planes)], load_sems.at[k])
        for k in range(fields)
    ]
    tables = [
        pltpu.make_async_copy(src, dst, table_sems.at[k])
        for k, (src, dst) in enumerate((
            (wall_tab.at[me_w], wall_t), (span_tab.at[me_s], span_t),
        ))
    ]
    for copy in tables[:1] + loads[:2] + tables[1:] + loads[2:]:
        copy.start()

    def device(axis, shift):
        if axis == 0:
            return (me_w + shift, me_s, me_c)
        return (me_w, me_s + shift, me_c)

    axes = ((0, me_w, wall_n), (1, me_s, span_n))
    barrier = pltpu.get_barrier_semaphore()
    for axis, me, n in axes:
        for d in range(1, n):
            @pl.when(me + d < n)
            def _():
                pl.semaphore_signal(barrier, inc=1, device_id=device(axis, d), device_id_type=MESH)

            @pl.when(me >= d)
            def _():
                pl.semaphore_signal(barrier, inc=1, device_id=device(axis, -d), device_id_type=MESH)

    wall_msg[...] = jnp.zeros_like(wall_msg)
    span_msg[...] = jnp.zeros_like(span_msg)
    outs, nears, fars = (wall_out, span_out), (wall_near, span_near), (wall_far, span_far)
    gains = (wall_gains, span_gains)

    def transfer(axis, side, d):
        if d == 1:
            src, dst = outs[axis].at[pl.ds(3 * side, 3)], nears[axis].at[side]
        else:
            src, dst = outs[axis].at[3 * side], fars[axis].at[side, d - 2]
        return pltpu.make_async_remote_copy(
            src_ref=src, dst_ref=dst,
            send_sem=send_sems.at[axis, side, d - 1], recv_sem=recv_sems.at[axis, side, d - 1],
            device_id=device(axis, d if side == 0 else -d), device_id_type=MESH,
        )

    def has_target(me, n, side, d):
        return me + d < n if side == 0 else me >= d

    def has_source(me, n, side, d):
        return me >= d if side == 0 else me + d < n

    def send_all(axis, me, n):
        for d in range(n - 1, 0, -1):
            for side in range(2):
                @pl.when(has_target(me, n, side, d))
                def _():
                    transfer(axis, side, d).start()

    tables[0].wait()
    columns_at = 2 * rows + 16
    picks = wall_t[:rows, columns_at : columns_at + 4].astype(jnp.float32)
    picks = picks[:, :2] + picks[:, 2:]
    wall_a = jnp.broadcast_to(picks[:, 0:1], (rows, columns))
    wall_b = jnp.broadcast_to(picks[:, 1:2], (rows, columns))
    for k in range(fields):
        loads[k].wait()
        here = pl.ds(k * planes, planes)
        values = f_buf[here]
        wall_out[0, here, :] = jnp.sum(values * wall_a[None], axis=1)
        wall_out[3, here, :] = jnp.sum(values * wall_b[None], axis=1)
        wall_out[1, here, :] = f_buf[here, rows - 2, :]
        wall_out[2, here, :] = f_buf[here, rows - 1, :]
        wall_out[4, here, :] = f_buf[here, 0, :]
        wall_out[5, here, :] = f_buf[here, 1, :]
    pl.semaphore_wait(barrier, wall_n + span_n - 2)
    send_all(*axes[0])

    tables[1].wait()
    tiles = planes * rows // 128
    depth = 2 * columns
    for k in range(fields):
        high, low = halves(f_buf[pl.ds(k * planes, planes)].reshape(planes * rows, columns))
        both = jnp.concatenate([high, low], axis=1)
        picked = lax.dot_general(
            span_t[depth : depth + 16], both, (((1,), (1,)), ((), ())), preferred_element_type=jnp.float32
        )
        picked = picked[:8] + picked[8:]
        for t in range(tiles):
            for m in range(6):
                span_out[m, k * tiles + t : k * tiles + t + 1, :] = picked[m : m + 1, t * 128 : (t + 1) * 128]
    send_all(*axes[1])

    wall_fix[...] = wall_t[:, 2 * rows : 2 * rows + 16]
    span_fix[...] = span_t[depth + 16 : depth + 32]
    group = 4

    @pl.loop(0, slabs // group)
    def _(step):
        here = pl.ds(step * group, group)
        high, low = halves(f_buf[here])
        both = jnp.concatenate([high, low], axis=2).reshape(group * rows, depth)
        spread = jnp.dot(both, span_t[:depth], preferred_element_type=jnp.float32)
        spread = spread[:, :columns] + spread[:, columns:]
        span_loc[here] = spread.reshape(group, rows, columns)
        for q in range(0, group, 2):
            pair = jnp.concatenate(
                [jnp.concatenate([high[j], low[j]], axis=0) for j in (q, q + 1)], axis=1
            )
            solved = jnp.dot(wall_t[:, : 2 * rows], pair, preferred_element_type=jnp.float32)
            solved = solved[:rows] + solved[rows:]
            wall_loc[step * group + q] = solved[:, :columns]
            wall_loc[step * group + q + 1] = solved[:, columns:]

    msgs = (wall_msg, span_msg)
    for axis, me, n in axes:
        for d in range(1, n):
            for side in range(2):
                @pl.when(has_source(me, n, side, d))
                def _():
                    transfer(axis, side, d).wait_recv()
                    gain = jnp.float32(0.0)
                    for p in range(n):
                        gain = jnp.where(me == p, jnp.float32(gains[axis][side, p, d - 1]), gain)
                    if d == 1:
                        msgs[axis][3 * side] += gain * nears[axis][side, 0]
                        msgs[axis][3 * side + 1] = nears[axis][side, 1]
                        msgs[axis][3 * side + 2] = nears[axis][side, 2]
                    else:
                        msgs[axis][3 * side] += gain * fars[axis][side, d - 2]
    for axis, me, n in axes:
        for d in range(1, n):
            for side in range(2):
                @pl.when(has_target(me, n, side, d))
                def _():
                    transfer(axis, side, d).wait_send()


def correct_kernel(
    group, wall_loc, span_loc, wall_metric, span_metric, wall_msg, span_msg, wall_fix, span_fix,
    wall_hbm, span_hbm, wall_buf, span_buf, sems,
):
    planes = wall_metric.shape[0]
    slabs, rows, columns = wall_loc.shape
    tiles = group * rows // 128
    parts = planes // group

    def copies(step):
        here = pl.ds(step * group, group)
        return (
            pltpu.make_async_copy(wall_buf.at[here], wall_hbm.at[here], sems.at[0, step]),
            pltpu.make_async_copy(span_buf.at[here], span_hbm.at[here], sems.at[1, step]),
        )

    @pl.loop(0, slabs // group)
    def _(step):
        here = pl.ds(step * group, group)
        plane = (step % parts) * group
        edge = jnp.concatenate([span_msg[:, step * tiles + t, :] for t in range(tiles)], axis=1)
        edge_high, edge_low = halves(edge)
        edges = jnp.concatenate([edge_high.astype(jnp.float32), edge_low.astype(jnp.float32)], axis=0).T
        spread = jnp.dot(edges.astype(jnp.bfloat16), span_fix[...], preferred_element_type=jnp.float32)
        spread = (spread[:, :columns] + spread[:, columns:]).reshape(group, rows, columns)
        span_buf[here] = (span_loc[here] + spread) * span_metric[pl.ds(plane, group)]
        for q in range(0, group, 2):
            msgs = [
                jnp.concatenate(halves(wall_msg[:, step * group + j, :]), axis=0) for j in (q, q + 1)
            ]
            solved = jnp.dot(wall_fix[...], jnp.concatenate(msgs, axis=1), preferred_element_type=jnp.float32)
            solved = solved[:rows] + solved[rows:]
            for j in range(2):
                wall_buf[step * group + q + j] = (
                    wall_loc[step * group + q + j] + solved[:, j * columns : (j + 1) * columns]
                ) * wall_metric[plane + q + j]
        for copy in copies(step):
            copy.start()

    @pl.loop(0, slabs // group)
    def _(step):
        for copy in copies(step):
            copy.wait()


def per_device(wall_n, span_n, conserved, wall_metric, span_metric):
    fields, planes, rows, columns = conserved.shape
    slabs = fields * planes
    lines = slabs * rows // 128
    own_w, fix_w, sends_w, gains_w = block_tables(wall_n, rows)
    own_s, fix_s, sends_s, gains_s = block_tables(span_n, columns)
    f32, bf16 = jnp.float32, jnp.bfloat16

    own_high, own_low = split(own_w)
    fix_high, fix_low = split(fix_w)
    picks = np.concatenate(split(sends_w[:, (0, 3)].transpose(0, 2, 1)), axis=2)
    wall_tab = np.concatenate([
        np.concatenate([own_high, own_high, fix_high, fix_high, picks], axis=2),
        np.concatenate([own_low, own_low, fix_low, fix_low, picks], axis=2),
    ], axis=1)
    own_high, own_low = split(own_s.transpose(0, 2, 1))
    sends_high, sends_low = split(sends_s)
    fix_high, fix_low = split(fix_s.transpose(0, 2, 1))
    span_tab = np.concatenate(
        [np.concatenate([own_high, own_low], axis=2)] * 2
        + [np.concatenate([t, t], axis=2) for t in (sends_high, sends_low)]
        + [np.concatenate([fix_high, fix_low], axis=2)] * 2,
        axis=1,
    )

    vmem = pl.BlockSpec(memory_space=pltpu.VMEM)
    hbm = pl.BlockSpec(memory_space=pltpu.HBM)
    far = max(wall_n, span_n) - 1
    flat = (slabs, rows, columns)
    local = pl.pallas_call(
        functools.partial(exchange_kernel, wall_n, span_n, gains_w, gains_s),
        out_shape=(
            jax.ShapeDtypeStruct(flat, f32),
            jax.ShapeDtypeStruct(flat, f32),
            jax.ShapeDtypeStruct((8, slabs, 128), f32),
            jax.ShapeDtypeStruct((8, lines, 128), f32),
            jax.ShapeDtypeStruct((2 * rows, 16), bf16),
            jax.ShapeDtypeStruct((16, 2 * columns), bf16),
        ),
        in_specs=[hbm] * 3,
        out_specs=(vmem,) * 6,
        scratch_shapes=[
            pltpu.VMEM(flat, f32),
            pltpu.VMEM(wall_tab.shape[1:], bf16),
            pltpu.VMEM(span_tab.shape[1:], bf16),
            pltpu.VMEM((6, slabs, 128), f32),
            pltpu.VMEM((6, lines, 128), f32),
            pltpu.VMEM((2, 3, slabs, 128), f32),
            pltpu.VMEM((2, 3, lines, 128), f32),
            pltpu.VMEM((2, max(wall_n - 2, 1), slabs, 128), f32),
            pltpu.VMEM((2, max(span_n - 2, 1), lines, 128), f32),
            pltpu.SemaphoreType.DMA((fields,)),
            pltpu.SemaphoreType.DMA((2,)),
            pltpu.SemaphoreType.DMA((2, 2, far)),
            pltpu.SemaphoreType.DMA((2, 2, far)),
        ],
        compiler_params=pltpu.CompilerParams(
            collective_id=0, has_side_effects=True, vmem_limit_bytes=43 * 1024 * 1024
        ),
        name="exchange",
    )(conserved, jnp.asarray(wall_tab), jnp.asarray(span_tab))

    group = 4
    outs = pl.pallas_call(
        functools.partial(correct_kernel, group),
        out_shape=(jax.ShapeDtypeStruct(flat, f32),) * 2,
        in_specs=[vmem] * 8,
        out_specs=(hbm, hbm),
        scratch_shapes=[
            pltpu.VMEM(flat, f32), pltpu.VMEM(flat, f32), pltpu.SemaphoreType.DMA((2, slabs // group)),
        ],
        compiler_params=pltpu.CompilerParams(vmem_limit_bytes=24 * 1024 * 1024),
        cost_estimate=pl.CostEstimate(
            flops=2 * slabs * rows * columns * 16 * 8, bytes_accessed=8 * conserved.size, transcendentals=0
        ),
        name="correct",
    )(local[0], local[1], wall_metric, span_metric, *local[2:])
    return tuple(out.reshape(conserved.shape) for out in outs)


def solution(mesh):
    in_specs = (
        P(None, "stream", "wall", "span"),
        P("stream", "wall", "span"),
        P("stream", "wall", "span"),
    )
    out_specs = (P(None, "stream", "wall", "span"), P(None, "stream", "wall", "span"))
    sizes = (mesh.shape["wall"], mesh.shape["span"])
    return jax.shard_map(
        functools.partial(per_device, *sizes), mesh=mesh, in_specs=in_specs, out_specs=out_specs, check_vma=False
    )
```

time: 28.2 us -> 22.9 us (0.81)
  local copies, waits for them, and re-layouts: 7.36 us -> 2.18 us
    unnamed x18 -> x8, local copies, waits for them, and re-layouts: 7.36 us -> 2.18 us
where the time goes in v2:
time: 22.9 us; the launch traced here: 22.7 us
  Pallas kernels  19.9 us (87%)
  local copies, waits for them, and re-layouts  2.18 us (10%)
  between operations  0.68 us (3%)
    pallas_call x1, Pallas kernels, per_device(): pl.pallas_call(functools.partial(exchange_kernel, wall_n, span_n, gains_w...  12.7 us
    pallas_call x1, Pallas kernels, per_device(): pl.pallas_call(functools.partial(correct_kernel, group), out_shape=(jax.S...  7.18 us
    unnamed x8, local copies, waits for them, and re-layouts  2.18 us

profile of v2, /device:TPU:0, one launch (start us, length us, event | category | flops | bytes accessed | tf_op | source)
XLA Modules:
  0.0 22.7 jit_solution(14767186609802035385)
XLA Ops:
  0.6 0.0 copy-start.1
  0.6 0.0 copy-start
  0.6 0.0 copy-start.2
  0.7 1.2 %copy-done.2 = bf16[4,288,256]{2,1,0:T(8,128)(2,1)S(1)} copy-done((bf16[4,288,256]{2,1,0:T(8,128)(2,1)S(1)}, bf16[4,288,256]{2,1,0:T(8,128)(2,1)}, u32[]{:S(2)}) %copy-start.2) | copy-done | bytes 589848
  1.8 0.0 copy-start.3
  1.8 1.0 %copy-done.3 = bf16[4,192,212]{2,1,0:T(8,128)(2,1)S(1)} copy-done((bf16[4,192,212]{2,1,0:T(8,128)(2,1)S(1)}, bf16[4,192,212]{2,1,0:T(8,128)(2,1)}, u32[]{:S(2)}) %copy-start.3) | copy-done | bytes 325656
  2.8 12.7 %exchange.1 = (f32[80,96,128]{2,1,0:T(8,128)S(1)}, f32[80,96,128]{2,1,0:T(8,128)S(1)}, f32[8,80,128]{2,1,0:T(8,128)S(1)}, f32[8,60,128]{2,1,0:T(8,128)S(1)}, bf1...) custom-call(f32[5,16,96,128]{3,2,1,0:T(8,128)} %f_hbm.1, bf16[4,192,212]{2,1,0:T(8,128)(2,1)S(1)} %copy-done.3, ...), custom_call_target="tpu_custom_call" | custom-call | tf_op jit(solution)/shard_map/exchange/pallas_call | solution.py:305
  15.5 0.0 copy-done.1
  15.5 0.0 copy-done
  15.6 7.2 %correct.1 = (f32[80,96,128]{2,1,0:T(8,128)}, f32[80,96,128]{2,1,0:T(8,128)}) custom-call(f32[80,96,128]{2,1,0:T(8,128)S(1)} %get-tuple-element.10.wall_loc, f32[80,96,128]{2,1,0:T(8,128)S(1)} %get-tuple-element.11.span_loc, f32[16,96,128]{2,1,0:T(8,128)S(1)} %copy-done, f32[16,96,128]{2,1,0:T(8,128)S(1)} %copy-done.1, ...), custom_call_target="tpu_custom_call" | custom-call | flops 251658240 | bytes 7864320 | tf_op jit(solution)/shard_map/correct/pallas_call | solution.py:339
Async XLA Ops:
  0.6 14.9 %copy-start.1 = (f32[16,96,128]{2,1,0:T(8,128)S(1)}, f32[16,96,128]{2,1,0:T(8,128)}, u32[]{:S(2)}) copy-start(f32[16,96,128]{2,1,0:T(8,128)} %span_metric.1) | copy-start | bytes 2359300
  0.6 14.9 %copy-start = (f32[16,96,128]{2,1,0:T(8,128)S(1)}, f32[16,96,128]{2,1,0:T(8,128)}, u32[]{:S(2)}) copy-start(f32[16,96,128]{2,1,0:T(8,128)} %wall_metric.1) | copy-start | bytes 2359300
  0.6 1.2 %copy-start.2 = (bf16[4,288,256]{2,1,0:T(8,128)(2,1)S(1)}, bf16[4,288,256]{2,1,0:T(8,128)(2,1)}, u32[]{:S(2)}) copy-start(bf16[4,288,256]{2,1,0:T(8,128)(2,1)} %constant.5.clone.span_tab) | copy-start | bytes 1769476
  1.8 1.0 %copy-start.3 = (bf16[4,192,212]{2,1,0:T(8,128)(2,1)S(1)}, bf16[4,192,212]{2,1,0:T(8,128)(2,1)}, u32[]{:S(2)}) copy-start(bf16[4,192,212]{2,1,0:T(8,128)(2,1)} %constant.4.clone.wall_tab) | copy-start | bytes 976900

commit v3 on v2

--- a/solution.py
+++ b/solution.py
@@ -74,6 +74,12 @@
     return high, low
 
 
+def roomy(table):
+    pieces, rows, width = table.shape
+    more = max(0, (1 << 21) // (pieces * max(width, 256)) - rows)
+    return jnp.asarray(np.pad(table, ((0, 0), (0, -(-more // 16) * 16), (0, 0))))
+
+
 def halves(values):
     high = values.astype(jnp.bfloat16)
     low = (values - high.astype(jnp.float32)).astype(jnp.bfloat16)
@@ -97,7 +103,8 @@
     tables = [
         pltpu.make_async_copy(src, dst, table_sems.at[k])
         for k, (src, dst) in enumerate((
-            (wall_tab.at[me_w], wall_t), (span_tab.at[me_s], span_t),
+            (wall_tab.at[me_w, pl.ds(0, wall_t.shape[0])], wall_t),
+            (span_tab.at[me_s, pl.ds(0, span_t.shape[0])], span_t),
         ))
     ]
     for copy in tables[:1] + loads[:2] + tables[1:] + loads[2:]:
@@ -187,22 +194,24 @@
     span_fix[...] = span_t[depth + 16 : depth + 32]
     group = 4
 
-    @pl.loop(0, slabs // group)
-    def _(step):
-        here = pl.ds(step * group, group)
-        high, low = halves(f_buf[here])
-        both = jnp.concatenate([high, low], axis=2).reshape(group * rows, depth)
-        spread = jnp.dot(both, span_t[:depth], preferred_element_type=jnp.float32)
-        spread = spread[:, :columns] + spread[:, columns:]
-        span_loc[here] = spread.reshape(group, rows, columns)
-        for q in range(0, group, 2):
-            pair = jnp.concatenate(
-                [jnp.concatenate([high[j], low[j]], axis=0) for j in (q, q + 1)], axis=1
-            )
-            solved = jnp.dot(wall_t[:, : 2 * rows], pair, preferred_element_type=jnp.float32)
-            solved = solved[:rows] + solved[rows:]
-            wall_loc[step * group + q] = solved[:, :columns]
-            wall_loc[step * group + q + 1] = solved[:, columns:]
+    @pl.loop(0, fields)
+    def _(field):
+        for part in range(planes // group):
+            first = field * planes + part * group
+            here = pl.ds(first, group)
+            high, low = halves(f_buf[here])
+            both = jnp.concatenate([high, low], axis=2).reshape(group * rows, depth)
+            spread = jnp.dot(both, span_t[:depth], preferred_element_type=jnp.float32)
+            spread = spread[:, :columns] + spread[:, columns:]
+            span_loc[here] = spread.reshape(group, rows, columns)
+            for q in range(0, group, 2):
+                pair = jnp.concatenate(
+                    [jnp.concatenate([high[j], low[j]], axis=0) for j in (q, q + 1)], axis=1
+                )
+                solved = jnp.dot(wall_t[:, : 2 * rows], pair, preferred_element_type=jnp.float32)
+                solved = solved[:rows] + solved[rows:]
+                wall_loc[first + q] = solved[:, :columns]
+                wall_loc[first + q + 1] = solved[:, columns:]
 
     msgs = (wall_msg, span_msg)
     for axis, me, n in axes:
@@ -235,41 +244,42 @@
     planes = wall_metric.shape[0]
     slabs, rows, columns = wall_loc.shape
     tiles = group * rows // 128
-    parts = planes // group
-
-    def copies(step):
-        here = pl.ds(step * group, group)
+    fields = slabs // planes
+
+    def copies(field):
+        here = pl.ds(field * planes, planes)
         return (
-            pltpu.make_async_copy(wall_buf.at[here], wall_hbm.at[here], sems.at[0, step]),
-            pltpu.make_async_copy(span_buf.at[here], span_hbm.at[here], sems.at[1, step]),
+            pltpu.make_async_copy(wall_buf.at[here], wall_hbm.at[here], sems.at[0, field]),
+            pltpu.make_async_copy(span_buf.at[here], span_hbm.at[here], sems.at[1, field]),
         )
 
-    @pl.loop(0, slabs // group)
-    def _(step):
-        here = pl.ds(step * group, group)
-        plane = (step % parts) * group
-        edge = jnp.concatenate([span_msg[:, step * tiles + t, :] for t in range(tiles)], axis=1)
-        edge_high, edge_low = halves(edge)
-        edges = jnp.concatenate([edge_high.astype(jnp.float32), edge_low.astype(jnp.float32)], axis=0).T
-        spread = jnp.dot(edges.astype(jnp.bfloat16), span_fix[...], preferred_element_type=jnp.float32)
-        spread = (spread[:, :columns] + spread[:, columns:]).reshape(group, rows, columns)
-        span_buf[here] = (span_loc[here] + spread) * span_metric[pl.ds(plane, group)]
-        for q in range(0, group, 2):
-            msgs = [
-                jnp.concatenate(halves(wall_msg[:, step * group + j, :]), axis=0) for j in (q, q + 1)
-            ]
-            solved = jnp.dot(wall_fix[...], jnp.concatenate(msgs, axis=1), preferred_element_type=jnp.float32)
-            solved = solved[:rows] + solved[rows:]
-            for j in range(2):
-                wall_buf[step * group + q + j] = (
-                    wall_loc[step * group + q + j] + solved[:, j * columns : (j + 1) * columns]
-                ) * wall_metric[plane + q + j]
-        for copy in copies(step):
+    @pl.loop(0, fields)
+    def _(field):
+        for part in range(planes // group):
+            plane = part * group
+            first = field * planes + plane
+            here = pl.ds(first, group)
+            tile = (field * (planes // group) + part) * tiles
+            edge = jnp.concatenate([span_msg[:, tile + t, :] for t in range(tiles)], axis=1)
+            edge_high, edge_low = halves(edge)
+            edges = jnp.concatenate([edge_high.astype(jnp.float32), edge_low.astype(jnp.float32)], axis=0).T
+            spread = jnp.dot(edges.astype(jnp.bfloat16), span_fix[...], preferred_element_type=jnp.float32)
+            spread = (spread[:, :columns] + spread[:, columns:]).reshape(group, rows, columns)
+            span_buf[here] = (span_loc[here] + spread) * span_metric[pl.ds(plane, group)]
+            for q in range(0, group, 2):
+                msgs = [jnp.concatenate(halves(wall_msg[:, first + j, :]), axis=0) for j in (q, q + 1)]
+                solved = jnp.dot(wall_fix[...], jnp.concatenate(msgs, axis=1), preferred_element_type=jnp.float32)
+                solved = solved[:rows] + solved[rows:]
+                for j in range(2):
+                    wall_buf[first + q + j] = (
+                        wall_loc[first + q + j] + solved[:, j * columns : (j + 1) * columns]
+                    ) * wall_metric[plane + q + j]
+        for copy in copies(field):
             copy.start()
 
-    @pl.loop(0, slabs // group)
-    def _(step):
-        for copy in copies(step):
+    @pl.loop(0, fields)
+    def _(field):
+        for copy in copies(field):
             copy.wait()
 
 
@@ -333,7 +343,7 @@
             collective_id=0, has_side_effects=True, vmem_limit_bytes=43 * 1024 * 1024
         ),
         name="exchange",
-    )(conserved, jnp.asarray(wall_tab), jnp.asarray(span_tab))
+    )(conserved, roomy(wall_tab), roomy(span_tab))
 
     group = 4
     outs = pl.pallas_call(
@@ -342,7 +352,7 @@
         in_specs=[vmem] * 8,
         out_specs=(hbm, hbm),
         scratch_shapes=[
-            pltpu.VMEM(flat, f32), pltpu.VMEM(flat, f32), pltpu.SemaphoreType.DMA((2, slabs // group)),
+            pltpu.VMEM(flat, f32), pltpu.VMEM(flat, f32), pltpu.SemaphoreType.DMA((2, fields)),
         ],
         compiler_params=pltpu.CompilerParams(vmem_limit_bytes=24 * 1024 * 1024),
         cost_estimate=pl.CostEstimate(

time: 22.9 us -> 17.6 us (0.77)
  Pallas kernels: 19.9 us -> 16.8 us
  local copies, waits for them, and re-layouts: 2.18 us -> 0.01 us
    pallas_call x1, Pallas kernels: 7.18 us -> 4.34 us  [per_device(): pl.pallas_call(functools.partial(correct_kernel, group), out_shape=(jax.S...]
    unnamed x8 -> x4, local copies, waits for them, and re-layouts: 2.18 us -> 0.01 us
    pallas_call x1, Pallas kernels: 12.7 us -> 12.4 us  [per_device(): pl.pallas_call(functools.partial(exchange_kernel, wall_n, span_n, gains_w...]
where the time goes in v3:
time: 17.6 us; the launch traced here: 17.4 us
  Pallas kernels  16.8 us (95%)
  between operations  0.67 us (4%)
    pallas_call x1, Pallas kernels, per_device(): pl.pallas_call(functools.partial(exchange_kernel, wall_n, span_n, gains_w...  12.4 us
    pallas_call x1, Pallas kernels, per_device(): pl.pallas_call(functools.partial(correct_kernel, group), out_shape=(jax.S...  4.34 us

profile of v3, /device:TPU:0, one launch (start us, length us, event | category | flops | bytes accessed | tf_op | source)
XLA Modules:
  0.0 17.4 jit_solution(16430195896019361392)
XLA Ops:
  0.6 0.0 copy-start.1
  0.6 0.0 copy-start
  0.6 12.4 %exchange.1 = (f32[80,96,128]{2,1,0:T(8,128)S(1)}, f32[80,96,128]{2,1,0:T(8,128)S(1)}, f32[8,80,128]{2,1,0:T(8,128)S(1)}, f32[8,60,128]{2,1,0:T(8,128)S(1)}, bf1...) custom-call(f32[5,16,96,128]{3,2,1,0:T(8,128)} %f_hbm.1, bf16[4,2048,212]{2,1,0:T(8,128)(2,1)} %constant.4.clone.wall_tab, ...), custom_call_target="tpu_custom_call" | custom-call | tf_op jit(solution)/shard_map/exchange/pallas_call | solution.py:315
  13.1 0.0 copy-done.1
  13.1 0.0 copy-done
  13.1 4.3 %correct.1 = (f32[80,96,128]{2,1,0:T(8,128)}, f32[80,96,128]{2,1,0:T(8,128)}) custom-call(f32[80,96,128]{2,1,0:T(8,128)S(1)} %get-tuple-element.10.wall_loc, f32[80,96,128]{2,1,0:T(8,128)S(1)} %get-tuple-element.11.span_loc, f32[16,96,128]{2,1,0:T(8,128)S(1)} %copy-done, f32[16,96,128]{2,1,0:T(8,128)S(1)} %copy-done.1, ...), custom_call_target="tpu_custom_call" | custom-call | flops 251658240 | bytes 7864320 | tf_op jit(solution)/shard_map/correct/pallas_call | solution.py:349
Async XLA Ops:
  0.6 12.5 %copy-start.1 = (f32[16,96,128]{2,1,0:T(8,128)S(1)}, f32[16,96,128]{2,1,0:T(8,128)}, u32[]{:S(2)}) copy-start(f32[16,96,128]{2,1,0:T(8,128)} %span_metric.1) | copy-start | bytes 2359300
  0.6 12.5 %copy-start = (f32[16,96,128]{2,1,0:T(8,128)S(1)}, f32[16,96,128]{2,1,0:T(8,128)}, u32[]{:S(2)}) copy-start(f32[16,96,128]{2,1,0:T(8,128)} %wall_metric.1) | copy-start | bytes 2359300

commit v4 on v3

--- a/solution.py
+++ b/solution.py
@@ -157,7 +157,7 @@
                     transfer(axis, side, d).start()
 
     tables[0].wait()
-    columns_at = 2 * rows + 16
+    columns_at = 2 * rows + 32
     picks = wall_t[:rows, columns_at : columns_at + 4].astype(jnp.float32)
     picks = picks[:, :2] + picks[:, 2:]
     wall_a = jnp.broadcast_to(picks[:, 0:1], (rows, columns))
@@ -172,46 +172,65 @@
         wall_out[2, here, :] = f_buf[here, rows - 1, :]
         wall_out[4, here, :] = f_buf[here, 0, :]
         wall_out[5, here, :] = f_buf[here, 1, :]
-    pl.semaphore_wait(barrier, wall_n + span_n - 2)
-    send_all(*axes[0])
-
     tables[1].wait()
     tiles = planes * rows // 128
     depth = 2 * columns
-    for k in range(fields):
-        high, low = halves(f_buf[pl.ds(k * planes, planes)].reshape(planes * rows, columns))
-        both = jnp.concatenate([high, low], axis=1)
-        picked = lax.dot_general(
-            span_t[depth : depth + 16], both, (((1,), (1,)), ((), ())), preferred_element_type=jnp.float32
-        )
-        picked = picked[:8] + picked[8:]
-        for t in range(tiles):
-            for m in range(6):
-                span_out[m, k * tiles + t : k * tiles + t + 1, :] = picked[m : m + 1, t * 128 : (t + 1) * 128]
+    group = 4
+
+    def span_functionals():
+        for k in range(fields):
+            high, low = halves(f_buf[pl.ds(k * planes, planes)].reshape(planes * rows, columns))
+            both = jnp.concatenate([high, low], axis=1)
+            picked = lax.dot_general(
+                span_t[depth : depth + 16], both, (((1,), (1,)), ((), ())), preferred_element_type=jnp.float32
+            )
+            picked = picked[:8] + picked[8:]
+            for t in range(tiles):
+                for m in range(6):
+                    span_out[m, k * tiles + t : k * tiles + t + 1, :] = picked[m : m + 1, t * 128 : (t + 1) * 128]
+
+    def local_products():
+        @pl.loop(0, fields)
+        def _(field):
+            for part in range(planes // group):
+                first = field * planes + part * group
+                here = pl.ds(first, group)
+                high, low = halves(f_buf[here])
+                both = jnp.concatenate([high, low], axis=2).reshape(group * rows, depth)
+                spread = jnp.dot(both, span_t[:depth], preferred_element_type=jnp.float32)
+                spread = spread[:, :columns] + spread[:, columns:]
+                span_loc[here] = spread.reshape(group, rows, columns)
+                for q in range(0, group, 2):
+                    pair = jnp.concatenate(
+                        [jnp.concatenate([high[j], low[j]], axis=0) for j in (q, q + 1)], axis=1
+                    )
+                    solved = jnp.dot(wall_t[:, : 2 * rows], pair, preferred_element_type=jnp.float32)
+                    solved = solved[:rows] + solved[rows:]
+                    wall_loc[first + q] = solved[:, :columns]
+                    wall_loc[first + q + 1] = solved[:, columns:]
+
+    early = 2 * me_w < wall_n
+
+    @pl.when(early)
+    def _():
+        span_functionals()
+        local_products()
+
+    pl.semaphore_wait(barrier, wall_n + span_n - 2)
+    send_all(*axes[0])
+
+    @pl.when(jnp.logical_not(early))
+    def _():
+        span_functionals()
+
     send_all(*axes[1])
 
-    wall_fix[...] = wall_t[:, 2 * rows : 2 * rows + 16]
-    span_fix[...] = span_t[depth + 16 : depth + 32]
-    group = 4
-
-    @pl.loop(0, fields)
-    def _(field):
-        for part in range(planes // group):
-            first = field * planes + part * group
-            here = pl.ds(first, group)
-            high, low = halves(f_buf[here])
-            both = jnp.concatenate([high, low], axis=2).reshape(group * rows, depth)
-            spread = jnp.dot(both, span_t[:depth], preferred_element_type=jnp.float32)
-            spread = spread[:, :columns] + spread[:, columns:]
-            span_loc[here] = spread.reshape(group, rows, columns)
-            for q in range(0, group, 2):
-                pair = jnp.concatenate(
-                    [jnp.concatenate([high[j], low[j]], axis=0) for j in (q, q + 1)], axis=1
-                )
-                solved = jnp.dot(wall_t[:, : 2 * rows], pair, preferred_element_type=jnp.float32)
-                solved = solved[:rows] + solved[rows:]
-                wall_loc[first + q] = solved[:, :columns]
-                wall_loc[first + q + 1] = solved[:, columns:]
+    @pl.when(jnp.logical_not(early))
+    def _():
+        local_products()
+
+    wall_fix[...] = wall_t[:rows, 2 * rows : 2 * rows + 32]
+    span_fix[...] = span_t[depth + 16 : depth + 48, :columns]
 
     msgs = (wall_msg, span_msg)
     for axis, me, n in axes:
@@ -262,14 +281,14 @@
             tile = (field * (planes // group) + part) * tiles
             edge = jnp.concatenate([span_msg[:, tile + t, :] for t in range(tiles)], axis=1)
             edge_high, edge_low = halves(edge)
-            edges = jnp.concatenate([edge_high.astype(jnp.float32), edge_low.astype(jnp.float32)], axis=0).T
-            spread = jnp.dot(edges.astype(jnp.bfloat16), span_fix[...], preferred_element_type=jnp.float32)
-            spread = (spread[:, :columns] + spread[:, columns:]).reshape(group, rows, columns)
+            edges = [edge_high.astype(jnp.float32), edge_low.astype(jnp.float32)] * 2
+            edges = jnp.concatenate(edges, axis=0).T.astype(jnp.bfloat16)
+            spread = jnp.dot(edges, span_fix[...], preferred_element_type=jnp.float32)
+            spread = spread.reshape(group, rows, columns)
             span_buf[here] = (span_loc[here] + spread) * span_metric[pl.ds(plane, group)]
             for q in range(0, group, 2):
-                msgs = [jnp.concatenate(halves(wall_msg[:, first + j, :]), axis=0) for j in (q, q + 1)]
+                msgs = [jnp.concatenate(halves(wall_msg[:, first + j, :]) * 2, axis=0) for j in (q, q + 1)]
                 solved = jnp.dot(wall_fix[...], jnp.concatenate(msgs, axis=1), preferred_element_type=jnp.float32)
-                solved = solved[:rows] + solved[rows:]
                 for j in range(2):
                     wall_buf[first + q + j] = (
                         wall_loc[first + q + j] + solved[:, j * columns : (j + 1) * columns]
@@ -295,8 +314,8 @@
     fix_high, fix_low = split(fix_w)
     picks = np.concatenate(split(sends_w[:, (0, 3)].transpose(0, 2, 1)), axis=2)
     wall_tab = np.concatenate([
-        np.concatenate([own_high, own_high, fix_high, fix_high, picks], axis=2),
-        np.concatenate([own_low, own_low, fix_low, fix_low, picks], axis=2),
+        np.concatenate([own_high, own_high, fix_high, fix_high, fix_low, fix_low, picks], axis=2),
+        np.concatenate([own_low, own_low, fix_high, fix_high, fix_low, fix_low, picks], axis=2),
     ], axis=1)
     own_high, own_low = split(own_s.transpose(0, 2, 1))
     sends_high, sends_low = split(sends_s)
@@ -304,7 +323,7 @@
     span_tab = np.concatenate(
         [np.concatenate([own_high, own_low], axis=2)] * 2
         + [np.concatenate([t, t], axis=2) for t in (sends_high, sends_low)]
-        + [np.concatenate([fix_high, fix_low], axis=2)] * 2,
+        + [np.concatenate([t, t], axis=2) for t in (fix_high, fix_high, fix_low, fix_low)],
         axis=1,
     )
 
@@ -319,8 +338,8 @@
             jax.ShapeDtypeStruct(flat, f32),
             jax.ShapeDtypeStruct((8, slabs, 128), f32),
             jax.ShapeDtypeStruct((8, lines, 128), f32),
-            jax.ShapeDtypeStruct((2 * rows, 16), bf16),
-            jax.ShapeDtypeStruct((16, 2 * columns), bf16),
+            jax.ShapeDtypeStruct((rows, 32), bf16),
+            jax.ShapeDtypeStruct((32, columns), bf16),
         ),
         in_specs=[hbm] * 3,
         out_specs=(vmem,) * 6,

time: 17.6 us -> 19.4 us (1.10)
  Pallas kernels: 16.8 us -> 18.5 us
    pallas_call x1, Pallas kernels: 12.4 us -> 14.9 us  [per_device(): pl.pallas_call(functools.partial(exchange_kernel, wall_n, span_n, gains_w...]
    pallas_call x1, Pallas kernels: 4.34 us -> 3.62 us  [per_device(): pl.pallas_call(functools.partial(correct_kernel, group), out_shape=(jax.S...]
where the time goes in v4:
time: 19.4 us; the launch traced here: 19.2 us
  Pallas kernels  18.5 us (95%)
  between operations  0.67 us (3%)
    pallas_call x1, Pallas kernels, per_device(): pl.pallas_call(functools.partial(exchange_kernel, wall_n, span_n, gains_w...  14.9 us
    pallas_call x1, Pallas kernels, per_device(): pl.pallas_call(functools.partial(correct_kernel, group), out_shape=(jax.S...  3.62 us

profile of v4, /device:TPU:0, one launch (start us, length us, event | category | flops | bytes accessed | tf_op | source)
XLA Modules:
  0.0 19.2 jit_solution(9790850513351009147)
XLA Ops:
  0.6 0.0 copy-start.1
  0.6 0.0 copy-start
  0.6 14.9 %exchange.1 = (f32[80,96,128]{2,1,0:T(8,128)S(1)}, f32[80,96,128]{2,1,0:T(8,128)S(1)}, f32[8,80,128]{2,1,0:T(8,128)S(1)}, f32[8,60,128]{2,1,0:T(8,128)S(1)}, bf1...) custom-call(f32[5,16,96,128]{3,2,1,0:T(8,128)} %f_hbm.1, bf16[4,2048,228]{2,1,0:T(8,128)(2,1)} %constant.4.clone.wall_tab, ...), custom_call_target="tpu_custom_call" | custom-call | tf_op jit(solution)/shard_map/exchange/pallas_call | solution.py:334
  15.6 0.0 copy-done.1
  15.6 0.0 copy-done
  15.6 3.6 %correct.1 = (f32[80,96,128]{2,1,0:T(8,128)}, f32[80,96,128]{2,1,0:T(8,128)}) custom-call(f32[80,96,128]{2,1,0:T(8,128)S(1)} %get-tuple-element.10.wall_loc, f32[80,96,128]{2,1,0:T(8,128)S(1)} %get-tuple-element.11.span_loc, f32[16,96,128]{2,1,0:T(8,128)S(1)} %copy-done, f32[16,96,128]{2,1,0:T(8,128)S(1)} %copy-done.1, ...), custom_call_target="tpu_custom_call" | custom-call | flops 251658240 | bytes 7864320 | tf_op jit(solution)/shard_map/correct/pallas_call | solution.py:368
Async XLA Ops:
  0.6 14.9 %copy-start.1 = (f32[16,96,128]{2,1,0:T(8,128)S(1)}, f32[16,96,128]{2,1,0:T(8,128)}, u32[]{:S(2)}) copy-start(f32[16,96,128]{2,1,0:T(8,128)} %span_metric.1) | copy-start | bytes 2359300
  0.6 14.9 %copy-start = (f32[16,96,128]{2,1,0:T(8,128)S(1)}, f32[16,96,128]{2,1,0:T(8,128)}, u32[]{:S(2)}) copy-start(f32[16,96,128]{2,1,0:T(8,128)} %wall_metric.1) | copy-start | bytes 2359300

commit v5 on v4

--- a/solution.py
+++ b/solution.py
@@ -165,14 +165,16 @@
     for k in range(fields):
         loads[k].wait()
         here = pl.ds(k * planes, planes)
-        values = f_buf[here]
-        wall_out[0, here, :] = jnp.sum(values * wall_a[None], axis=1)
-        wall_out[3, here, :] = jnp.sum(values * wall_b[None], axis=1)
+        sums = [jnp.zeros((planes, 8, columns), jnp.float32)] * 2
+        for r in range(0, rows, 8):
+            values = f_buf[here, r : r + 8, :]
+            sums = [total + values * v[None, r : r + 8] for total, v in zip(sums, (wall_a, wall_b))]
+        wall_out[0, here, :] = jnp.sum(sums[0], axis=1)
+        wall_out[3, here, :] = jnp.sum(sums[1], axis=1)
         wall_out[1, here, :] = f_buf[here, rows - 2, :]
         wall_out[2, here, :] = f_buf[here, rows - 1, :]
         wall_out[4, here, :] = f_buf[here, 0, :]
         wall_out[5, here, :] = f_buf[here, 1, :]
-    tables[1].wait()
     tiles = planes * rows // 128
     depth = 2 * columns
     group = 4
@@ -209,25 +211,12 @@
                     wall_loc[first + q] = solved[:, :columns]
                     wall_loc[first + q + 1] = solved[:, columns:]
 
-    early = 2 * me_w < wall_n
-
-    @pl.when(early)
-    def _():
-        span_functionals()
-        local_products()
-
     pl.semaphore_wait(barrier, wall_n + span_n - 2)
     send_all(*axes[0])
-
-    @pl.when(jnp.logical_not(early))
-    def _():
-        span_functionals()
-
+    tables[1].wait()
+    span_functionals()
     send_all(*axes[1])
-
-    @pl.when(jnp.logical_not(early))
-    def _():
-        local_products()
+    local_products()
 
     wall_fix[...] = wall_t[:rows, 2 * rows : 2 * rows + 32]
     span_fix[...] = span_t[depth + 16 : depth + 48, :columns]

time: 19.4 us -> 16.9 us (0.87)
  Pallas kernels: 18.5 us -> 16 us
    pallas_call x1, Pallas kernels: 14.9 us -> 12.4 us  [per_device(): pl.pallas_call(functools.partial(exchange_kernel, wall_n, span_n, gains_w...]
where the time goes in v5:
time: 16.9 us; the launch traced here: 16.7 us
  Pallas kernels  16 us (95%)
  between operations  0.67 us (4%)
    pallas_call x1, Pallas kernels, per_device(): pl.pallas_call(functools.partial(exchange_kernel, wall_n, span_n, gains_w...  12.4 us
    pallas_call x1, Pallas kernels, per_device(): pl.pallas_call(functools.partial(correct_kernel, group), out_shape=(jax.S...  3.62 us

profile of v5, /device:TPU:0, one launch (start us, length us, event | category | flops | bytes accessed | tf_op | source)
XLA Modules:
  0.0 16.7 jit_solution(3040143139382112293)
XLA Ops:
  0.6 0.0 copy-start.1
  0.6 0.0 copy-start
  0.6 12.4 %exchange.1 = (f32[80,96,128]{2,1,0:T(8,128)S(1)}, f32[80,96,128]{2,1,0:T(8,128)S(1)}, f32[8,80,128]{2,1,0:T(8,128)S(1)}, f32[8,60,128]{2,1,0:T(8,128)S(1)}, bf1...) custom-call(f32[5,16,96,128]{3,2,1,0:T(8,128)} %f_hbm.1, bf16[4,2048,228]{2,1,0:T(8,128)(2,1)} %constant.4.clone.wall_tab, ...), custom_call_target="tpu_custom_call" | custom-call | tf_op jit(solution)/shard_map/exchange/pallas_call | solution.py:323
  13.1 0.0 copy-done.1
  13.1 0.0 copy-done
  13.1 3.6 %correct.1 = (f32[80,96,128]{2,1,0:T(8,128)}, f32[80,96,128]{2,1,0:T(8,128)}) custom-call(f32[80,96,128]{2,1,0:T(8,128)S(1)} %get-tuple-element.10.wall_loc, f32[80,96,128]{2,1,0:T(8,128)S(1)} %get-tuple-element.11.span_loc, f32[16,96,128]{2,1,0:T(8,128)S(1)} %copy-done, f32[16,96,128]{2,1,0:T(8,128)S(1)} %copy-done.1, ...), custom_call_target="tpu_custom_call" | custom-call | flops 251658240 | bytes 7864320 | tf_op jit(solution)/shard_map/correct/pallas_call | solution.py:357
Async XLA Ops:
  0.6 12.5 %copy-start.1 = (f32[16,96,128]{2,1,0:T(8,128)S(1)}, f32[16,96,128]{2,1,0:T(8,128)}, u32[]{:S(2)}) copy-start(f32[16,96,128]{2,1,0:T(8,128)} %span_metric.1) | copy-start | bytes 2359300
  0.6 12.5 %copy-start = (f32[16,96,128]{2,1,0:T(8,128)S(1)}, f32[16,96,128]{2,1,0:T(8,128)}, u32[]{:S(2)}) copy-start(f32[16,96,128]{2,1,0:T(8,128)} %wall_metric.1) | copy-start | bytes 2359300

commit v6 on v5

--- a/solution.py
+++ b/solution.py
@@ -133,24 +133,28 @@
     gains = (wall_gains, span_gains)
 
     def transfer(axis, side, d):
-        if d == 1:
-            src, dst = outs[axis].at[pl.ds(3 * side, 3)], nears[axis].at[side]
+        slot = d - 1 if d else send_sems.shape[2] - 1
+        if d == 0:
+            src, dst = outs[axis].at[pl.ds(3 * side + 1, 2)], nears[axis].at[side, pl.ds(1, 2)]
+            d = 1
+        elif d == 1:
+            src, dst = outs[axis].at[3 * side], nears[axis].at[side, 0]
         else:
             src, dst = outs[axis].at[3 * side], fars[axis].at[side, d - 2]
         return pltpu.make_async_remote_copy(
             src_ref=src, dst_ref=dst,
-            send_sem=send_sems.at[axis, side, d - 1], recv_sem=recv_sems.at[axis, side, d - 1],
+            send_sem=send_sems.at[axis, side, slot], recv_sem=recv_sems.at[axis, side, slot],
             device_id=device(axis, d if side == 0 else -d), device_id_type=MESH,
         )
 
     def has_target(me, n, side, d):
-        return me + d < n if side == 0 else me >= d
+        return me + max(d, 1) < n if side == 0 else me >= max(d, 1)
 
     def has_source(me, n, side, d):
         return me >= d if side == 0 else me + d < n
 
-    def send_all(axis, me, n):
-        for d in range(n - 1, 0, -1):
+    def send_all(axis, me, n, distances):
+        for d in distances:
             for side in range(2):
                 @pl.when(has_target(me, n, side, d))
                 def _():
@@ -165,16 +169,20 @@
     for k in range(fields):
         loads[k].wait()
         here = pl.ds(k * planes, planes)
+        wall_out[1, here, :] = f_buf[here, rows - 2, :]
+        wall_out[2, here, :] = f_buf[here, rows - 1, :]
+        wall_out[4, here, :] = f_buf[here, 0, :]
+        wall_out[5, here, :] = f_buf[here, 1, :]
+    pl.semaphore_wait(barrier, wall_n + span_n - 2)
+    send_all(*axes[0], (0,))
+    for k in range(fields):
+        here = pl.ds(k * planes, planes)
         sums = [jnp.zeros((planes, 8, columns), jnp.float32)] * 2
         for r in range(0, rows, 8):
             values = f_buf[here, r : r + 8, :]
             sums = [total + values * v[None, r : r + 8] for total, v in zip(sums, (wall_a, wall_b))]
         wall_out[0, here, :] = jnp.sum(sums[0], axis=1)
         wall_out[3, here, :] = jnp.sum(sums[1], axis=1)
-        wall_out[1, here, :] = f_buf[here, rows - 2, :]
-        wall_out[2, here, :] = f_buf[here, rows - 1, :]
-        wall_out[4, here, :] = f_buf[here, 0, :]
-        wall_out[5, here, :] = f_buf[here, 1, :]
     tiles = planes * rows // 128
     depth = 2 * columns
     group = 4
@@ -211,11 +219,10 @@
                     wall_loc[first + q] = solved[:, :columns]
                     wall_loc[first + q + 1] = solved[:, columns:]
 
-    pl.semaphore_wait(barrier, wall_n + span_n - 2)
-    send_all(*axes[0])
+    send_all(*axes[0], range(wall_n - 1, 0, -1))
     tables[1].wait()
     span_functionals()
-    send_all(*axes[1])
+    send_all(*axes[1], range(span_n - 1, -1, -1))
     local_products()
 
     wall_fix[...] = wall_t[:rows, 2 * rows : 2 * rows + 32]
@@ -228,6 +235,8 @@
                 @pl.when(has_source(me, n, side, d))
                 def _():
                     transfer(axis, side, d).wait_recv()
+                    if d == 1:
+                        transfer(axis, side, 0).wait_recv()
                     gain = jnp.float32(0.0)
                     for p in range(n):
                         gain = jnp.where(me == p, jnp.float32(gains[axis][side, p, d - 1]), gain)
@@ -238,7 +247,7 @@
                     else:
                         msgs[axis][3 * side] += gain * fars[axis][side, d - 2]
     for axis, me, n in axes:
-        for d in range(1, n):
+        for d in range(n):
             for side in range(2):
                 @pl.when(has_target(me, n, side, d))
                 def _():
@@ -344,8 +353,8 @@
             pltpu.VMEM((2, max(span_n - 2, 1), lines, 128), f32),
             pltpu.SemaphoreType.DMA((fields,)),
             pltpu.SemaphoreType.DMA((2,)),
-            pltpu.SemaphoreType.DMA((2, 2, far)),
-            pltpu.SemaphoreType.DMA((2, 2, far)),
+            pltpu.SemaphoreType.DMA((2, 2, far + 1)),
+            pltpu.SemaphoreType.DMA((2, 2, far + 1)),
         ],
         compiler_params=pltpu.CompilerParams(
             collective_id=0, has_side_effects=True, vmem_limit_bytes=43 * 1024 * 1024

time: 16.9 us -> 17.8 us (1.053)
  Pallas kernels: 16 us -> 17 us
    pallas_call x1, Pallas kernels: 12.4 us -> 13.4 us  [per_device(): pl.pallas_call(functools.partial(exchange_kernel, wall_n, span_n, gains_w...]
where the time goes in v6:
time: 17.8 us; the launch traced here: 17.6 us
  Pallas kernels  17 us (96%)
  between operations  0.67 us (4%)
    pallas_call x1, Pallas kernels, per_device(): pl.pallas_call(functools.partial(exchange_kernel, wall_n, span_n, gains_w...  13.4 us
    pallas_call x1, Pallas kernels, per_device(): pl.pallas_call(functools.partial(correct_kernel, group), out_shape=(jax.S...  3.62 us

profile of v6, /device:TPU:0, one launch (start us, length us, event | category | flops | bytes accessed | tf_op | source)
XLA Modules:
  0.0 17.6 jit_solution(16198993308895333208)
XLA Ops:
  0.6 0.0 copy-start.1
  0.6 0.0 copy-start
  0.6 13.4 %exchange.1 = (f32[80,96,128]{2,1,0:T(8,128)S(1)}, f32[80,96,128]{2,1,0:T(8,128)S(1)}, f32[8,80,128]{2,1,0:T(8,128)S(1)}, f32[8,60,128]{2,1,0:T(8,128)S(1)}, bf1...) custom-call(f32[5,16,96,128]{3,2,1,0:T(8,128)} %f_hbm.1, bf16[4,2048,228]{2,1,0:T(8,128)(2,1)} %constant.4.clone.wall_tab, ...), custom_call_target="tpu_custom_call" | custom-call | tf_op jit(solution)/shard_map/exchange/pallas_call | solution.py:332
  14.0 0.0 copy-done.1
  14.0 0.0 copy-done
  14.0 3.6 %correct.1 = (f32[80,96,128]{2,1,0:T(8,128)}, f32[80,96,128]{2,1,0:T(8,128)}) custom-call(f32[80,96,128]{2,1,0:T(8,128)S(1)} %get-tuple-element.10.wall_loc, f32[80,96,128]{2,1,0:T(8,128)S(1)} %get-tuple-element.11.span_loc, f32[16,96,128]{2,1,0:T(8,128)S(1)} %copy-done, f32[16,96,128]{2,1,0:T(8,128)S(1)} %copy-done.1, ...), custom_call_target="tpu_custom_call" | custom-call | flops 251658240 | bytes 7864320 | tf_op jit(solution)/shard_map/correct/pallas_call | solution.py:366
Async XLA Ops:
  0.6 13.4 %copy-start.1 = (f32[16,96,128]{2,1,0:T(8,128)S(1)}, f32[16,96,128]{2,1,0:T(8,128)}, u32[]{:S(2)}) copy-start(f32[16,96,128]{2,1,0:T(8,128)} %span_metric.1) | copy-start | bytes 2359300
  0.6 13.4 %copy-start = (f32[16,96,128]{2,1,0:T(8,128)S(1)}, f32[16,96,128]{2,1,0:T(8,128)}, u32[]{:S(2)}) copy-start(f32[16,96,128]{2,1,0:T(8,128)} %wall_metric.1) | copy-start | bytes 2359300
